TPU v7x, 512 devices: a whole 4x8x8 slice. The times are simulated.
512 devices in a mesh: src: 16 (over y_hi, x, core), dst: 32 (over z, y_lo).
Axes of the slice: x: 4, y: 8 (y_hi: 2, y_lo: 4; y = y_hi * 4 + y_lo), z: 8, core: 2. Of those that a mesh axis runs over, the one named last changes fastest.
Arguments:
- source_embedding_table: float32 [16, 32, 128, 384], P('src', 'dst'), may hold values from -1.75 to 1.75
- source_adagrad_state: float32 [16, 32, 128], P('src', 'dst'), may hold values from 0.001 to 0.1
- destination_embedding_table: float32 [16, 32, 128, 384], P('src', 'dst'), may hold values from -1.75 to 1.75
- destination_adagrad_state: float32 [16, 32, 128], P('src', 'dst'), may hold values from 0.001 to 0.1
- relations: float32 [2048, 384], replicated, may hold values from -6 to 6
- rel_state: float32 [2048], P(('src', 'dst')), may hold values from 0.001 to 0.1
- source_edge_rows: int32 [16, 32, 3, 256], P('src', 'dst'), may hold values from 0 to 127
- destination_edge_rows: int32 [16, 32, 3, 256], P('src', 'dst'), may hold values from 0 to 127
- edge_relation_index: int32 [16, 32, 3, 256], P('src', 'dst'), may hold values from 0 to 2047
- negative_block_rows: int32 [16, 32, 3, 2, 128], P('src', 'dst'), may hold values from 0 to 127
- bucket_block_counts: int32 [16, 32, 3], P('src', 'dst'), may hold values from 1 to 2
Outputs:
- src_out: float32 [16, 32, 128, 384], P('src', 'dst')
- src_state_out: float32 [16, 32, 128], P('src', 'dst')
- dst_out: float32 [16, 32, 128, 384], P('src', 'dst')
- dst_state_out: float32 [16, 32, 128], P('src', 'dst')
- rel_out: float32 [2048, 384], P(('src', 'dst'))
- rel_state_out: float32 [2048], P(('src', 'dst'))
All inputs are finite; a program needn't handle non-finite values.
Results may differ from a plain program's by a relative error of at most 0.0004.
Values sent between devices are 32-bit elements; how exact they have to be, the bound alone decides.
A program may use at most 64 MiB of HBM per device.

v0:
```python
import jax
import jax.numpy as jnp
from jax import lax
from jax.sharding import PartitionSpec as P


def shifted(block, axis, distance):
    devices = range(lax.axis_size(axis))
    route = [((i - distance) % len(devices), i) for i in devices]
    return lax.ppermute(block, axis, route)


def adagrad_update(block, state, grad):
    new_state = state + jnp.mean(grad * grad, axis=-1)
    return (block - 0.1 * grad / jnp.sqrt(new_state)[:, None], new_state)


def group_terms(c, carry, src_blk, dst_blk, relations, s_rows, d_rows, r_ids, negs):
    grad_src, grad_dst, grad_rel = carry
    start = c * 128
    s_idx = lax.dynamic_slice_in_dim(s_rows, start, 128)
    d_idx = lax.dynamic_slice_in_dim(d_rows, start, 128)
    r_idx = lax.dynamic_slice_in_dim(r_ids, start, 128)
    n_idx = lax.dynamic_index_in_dim(negs, c, 0, keepdims=False)
    src_vec = src_blk[s_idx]
    dst_vec = dst_blk[d_idx]
    rel_vec = relations[r_idx]
    product = src_vec * rel_vec
    prod_low = product.astype(jnp.bfloat16)
    neg_low = dst_blk[n_idx].astype(jnp.bfloat16)
    positive = jnp.sum(product * dst_vec, axis=-1)
    scores = lax.dot_general(
        prod_low, neg_low, (((1,), (1,)), ((), ())), preferred_element_type=jnp.float32
    )
    grad_pos = -jax.nn.sigmoid(-positive)
    grad_neg = (jax.nn.sigmoid(scores) / neg_low.shape[0]).astype(jnp.bfloat16)
    grad_prod = grad_pos[:, None] * dst_vec + jnp.dot(
        grad_neg, neg_low, preferred_element_type=jnp.float32
    )
    grad_negrows = lax.dot_general(
        grad_neg, prod_low, (((0,), (0,)), ((), ())), preferred_element_type=jnp.float32
    )
    grad_src = grad_src.at[s_idx].add(grad_prod * rel_vec)
    grad_dst = grad_dst.at[d_idx].add(grad_pos[:, None] * product).at[n_idx].add(grad_negrows)
    grad_rel = grad_rel.at[r_idx].add(grad_prod * src_vec)
    return (grad_src, grad_dst, grad_rel)


def on_device(
    source_embedding_table,
    source_adagrad_state,
    destination_embedding_table,
    destination_adagrad_state,
    relations,
    rel_state,
    source_edge_rows,
    destination_edge_rows,
    edge_relation_index,
    negative_block_rows,
    bucket_block_counts,
):
    src_blk, src_st = (source_embedding_table[0, 0], source_adagrad_state[0, 0])
    dst_blk, dst_st = (destination_embedding_table[0, 0], destination_adagrad_state[0, 0])
    grad_rel = jnp.zeros(relations.shape, jnp.float32)
    zeros = jnp.zeros(src_blk.shape, jnp.float32)
    for iteration_index in range(source_edge_rows.shape[2]):
        s_rows = source_edge_rows[0, 0, iteration_index]
        d_rows = destination_edge_rows[0, 0, iteration_index]
        r_ids = edge_relation_index[0, 0, iteration_index]
        negs = negative_block_rows[0, 0, iteration_index]
        live = bucket_block_counts[0, 0, iteration_index]
        s_cur, d_cur = (src_blk, dst_blk)

        def turn(c, carry):
            return group_terms(c, carry, s_cur, d_cur, relations, s_rows, d_rows, r_ids, negs)

        grad_src, grad_dst, grad_rel = lax.fori_loop(
            jnp.int32(0), live, turn, (zeros, zeros, grad_rel)
        )
        src_blk, src_st = adagrad_update(src_blk, src_st, grad_src)
        dst_blk, dst_st = adagrad_update(dst_blk, dst_st, grad_dst)
        src_blk, src_st = shifted((src_blk, src_st), "src", 1)
        dst_blk, dst_st = shifted((dst_blk, dst_st), "dst", 1)
    share = rel_state.shape[0]
    first = lax.axis_index(("src", "dst")) * share
    total = lax.psum(grad_rel, ("src", "dst"))
    own_grad = lax.dynamic_slice_in_dim(total, first, share, 0)
    own_rel = lax.dynamic_slice_in_dim(relations, first, share, 0)
    updated_relation, updated_relation_state = adagrad_update(own_rel, rel_state, own_grad)
    return (
        src_blk[None, None],
        src_st[None, None],
        dst_blk[None, None],
        dst_st[None, None],
        updated_relation,
        updated_relation_state,
    )


def solution(mesh):
    in_specs = (
        P("src", "dst", None, None),
        P("src", "dst", None),
        P("src", "dst", None, None),
        P("src", "dst", None),
        P(),
        P(("src", "dst")),
        P("src", "dst", None, None),
        P("src", "dst", None, None),
        P("src", "dst", None, None),
        P("src", "dst", None, None, None),
        P("src", "dst", None),
    )
    out_specs = (
        P("src", "dst", None, None),
        P("src", "dst", None),
        P("src", "dst", None, None),
        P("src", "dst", None),
        P(("src", "dst"), None),
        P(("src", "dst")),
    )
    return jax.shard_map(
        on_device, mesh=mesh, in_specs=in_specs, out_specs=out_specs, check_vma=False
    )
```

profile of v0, /device:TPU:6, one launch (start us, length us, event | category | flops | bytes accessed | tf_op | source)
XLA Modules:
  0.0 442.8 jit_solution(12691013858704359464)
XLA Ops:
  7.2 1.4 fusion.64
  11.5 1.9 broadcast_in_dim.51
  13.4 16.7 %while.42 = (s32[]{:T(128)}, f32[128,384]{1,0:T(8,128)S(1)}, f32[128,384]{1,0:T(8,128)S(1)}, f32[2048,384]{1,0:T(8,128)}, s32[]{:T(128)}, /*index=5*/s32[256]{0:...) while((s32[]{:T(128)}, f32[128,384]{1,0:T(8,128)S(1)}, ...), condition=%wide.region_6.7_spmd, body=%wide.region_0.6_spmd.sunk | while | flops 38524680 | bytes 8580353 | solution.py:77
  16.6 2.7 gather_fusion.3
  19.9 1.5 scatter_custom_fusion.45
  21.4 1.5 scatter_custom_fusion.46
  23.1 1.4 scatter_fusion
  24.6 4.9 %scatter_custom_fusion.48 = f32[2048,384]{1,0:T(8,128)} fusion(f32[2048,384]{1,0:T(8,128)} %get-tuple-element.589, s32[128]{0:T(128)S(1)} %get-tuple-element.534, f32[128,384]{1,0:T(8,128)S(1)} %convolution_add_fusion.6, f32[128,384]{1,0:T(8,128)S(1)} %gather_fusion.2), kind=kCustom, calls=%fused_computation.31.clone.1 | custom fusion | flops 98304 | bytes 3538944 | tf_op jit(solution)/shard_map/while/body/scatter-add | solution.py:45
  30.3 1.9 collective-permute-start
  32.5 3.5 collective-permute-start.1
  36.0 6.6 %collective-permute-start.2 = (f32[128]{0:T(128)S(1)}, f32[128]{0:T(128)S(1)}, u32[]{:S(2)}, u32[]{:S(2)}) collective-permute-start(f32[128]{0:T(128)S(1)} %get-tuple-element.301), channel_id=1, source_target_pairs={{480,0},{0,32},{32,64},{64,96},{96,128},{128,160},{160,192},{192,2... | collective-permute-start | bytes 1544 | tf_op jit(solution)/shard_map/ppermute | solution.py:10
  42.6 18.6 %collective-permute-start.4 = (f32[128]{0:T(128)S(1)}, f32[128]{0:T(128)S(1)}, u32[]{:S(2)}, u32[]{:S(2)}) collective-permute-start(f32[128]{0:T(128)S(1)} %get-tuple-element.299), channel_id=1, source_target_pairs={{31,0},{0,1},{1,2},{2,3},{3,4},{4,5},{5,6},{6,7},{7,8},{8,9},{9,10... | collective-permute-start | bytes 1544 | tf_op jit(solution)/shard_map/ppermute | solution.py:10
  61.2 7.7 %collective-permute-done.1 = f32[128,384]{1,0:T(8,128)S(1)} collective-permute-done((f32[128,384]{1,0:T(8,128)S(1)}, f32[128,384]{1,0:T(8,128)S(1)}, u32[]{:S(2)}, u32[]{:S(2)}) %collective-permute-start.1) | collective-permute-done | bytes 196640 | tf_op jit(solution)/shard_map/ppermute | solution.py:10
  69.0 16.7 %while.43 = (s32[]{:T(128)}, f32[128,384]{1,0:T(8,128)S(1)}, f32[128,384]{1,0:T(8,128)S(1)}, f32[2048,384]{1,0:T(8,128)}, s32[]{:T(128)}, /*index=5*/s32[256]{0:...) while((s32[]{:T(128)}, f32[128,384]{1,0:T(8,128)S(1)}, ...), condition=%wide.region_15.16_spmd, body=%wide.region_9.15_spmd.sunk | while | flops 38524680 | bytes 8580353 | solution.py:77
  69.7 0.8 gather_fusion.4
  72.2 2.7 gather_fusion.7
  75.4 1.5 scatter_custom_fusion.52
  76.9 1.5 scatter_custom_fusion.53
  78.6 1.4 scatter_fusion.1
  80.1 4.9 %scatter_custom_fusion.55 = f32[2048,384]{1,0:T(8,128)} fusion(f32[2048,384]{1,0:T(8,128)} %get-tuple-element.640, s32[128]{0:T(128)S(1)} %get-tuple-element.550, f32[128,384]{1,0:T(8,128)S(1)} %convolution_add_fusion.7, f32[128,384]{1,0:T(8,128)S(1)} %gather_fusion.6), kind=kCustom, calls=%fused_computation.61.clone.1 | custom fusion | flops 98304 | bytes 3538944 | tf_op jit(solution)/shard_map/while/body/scatter-add | solution.py:45
  85.9 1.9 collective-permute-start.3
  88.0 10.5 %collective-permute-start.5 = (f32[128,384]{1,0:T(8,128)S(1)}, f32[128,384]{1,0:T(8,128)S(1)}, u32[]{:S(2)}, u32[]{:S(2)}) collective-permute-start(f32[128,384]{1,0:T(8,128)S(1)} %divide_subtract_fusion.2), channel_id=1, source_target_pairs={{31,0},{0,1},{1,2},{2,3},{3,4},{4,5},{5,6},{6,7},{7,8},{8,9},{9,10... | collective-permute-start | bytes 589832 | tf_op jit(solution)/shard_map/ppermute | solution.py:10
  98.6 14.0 %collective-permute-done.5 = f32[128,384]{1,0:T(8,128)S(1)} collective-permute-done((f32[128,384]{1,0:T(8,128)S(1)}, f32[128,384]{1,0:T(8,128)S(1)}, u32[]{:S(2)}, u32[]{:S(2)}) %collective-permute-start.5) | collective-permute-done | bytes 196640 | tf_op jit(solution)/shard_map/ppermute | solution.py:10
  112.6 32.9 %while.44 = (s32[]{:T(128)}, f32[128,384]{1,0:T(8,128)S(1)}, f32[128,384]{1,0:T(8,128)S(1)}, f32[2048,384]{1,0:T(8,128)}, s32[]{:T(128)}, /*index=5*/s32[256]{0:...) while((s32[]{:T(128)}, f32[128,384]{1,0:T(8,128)S(1)}, ...), condition=%wide.region_24.25_spmd, body=%wide.region_18.24_spmd.sunk | while | flops 38524680 | bytes 8580353 | solution.py:77
  116.0 2.7 gather_fusion.11
  119.3 1.5 scatter_custom_fusion.59
  120.7 1.5 scatter_custom_fusion.60
  122.5 1.4 scatter_fusion.2
  123.9 4.9 %scatter_custom_fusion.62 = f32[2048,384]{1,0:T(8,128)} fusion(f32[2048,384]{1,0:T(8,128)} %get-tuple-element.691, s32[128]{0:T(128)S(1)} %get-tuple-element.566, f32[128,384]{1,0:T(8,128)S(1)} %convolution_add_fusion.8, f32[128,384]{1,0:T(8,128)S(1)} %gather_fusion.10), kind=kCustom, calls=%fused_computation.91.clone.1 | custom fusion | flops 98304 | bytes 3538944 | tf_op jit(solution)/shard_map/while/body/scatter-add | solution.py:45
  129.6 0.8 gather_fusion.8
  132.0 2.7 gather_fusion.11
  135.3 1.5 scatter_custom_fusion.59
  136.7 1.5 scatter_custom_fusion.60
  138.5 1.4 scatter_fusion.2
  139.9 4.9 %scatter_custom_fusion.62 = f32[2048,384]{1,0:T(8,128)} fusion(f32[2048,384]{1,0:T(8,128)} %get-tuple-element.691, s32[128]{0:T(128)S(1)} %get-tuple-element.566, f32[128,384]{1,0:T(8,128)S(1)} %convolution_add_fusion.8, f32[128,384]{1,0:T(8,128)S(1)} %gather_fusion.10), kind=kCustom, calls=%fused_computation.91.clone.1 | custom fusion | flops 98304 | bytes 3538944 | tf_op jit(solution)/shard_map/while/body/scatter-add | solution.py:45
  145.5 1.9 collective-permute-start.6
  147.5 1.9 collective-permute-start.9
  149.5 0.9 collective-permute-done.6
  150.5 1.9 collective-permute-start.7
  152.5 4.3 collective-permute-done.9
  156.9 1.9 collective-permute-start.10
  158.8 1.9 collective-permute-start.8
  160.8 1.9 collective-permute-start.11
  162.7 1.0 collective-permute-done.8
  163.7 7.7 %collective-permute-done.11 = f32[128]{0:T(128)S(1)} collective-permute-done((f32[128]{0:T(128)S(1)}, f32[128]{0:T(128)S(1)}, u32[]{:S(2)}, u32[]{:S(2)}) %collective-permute-start.11) | collective-permute-done | bytes 544 | tf_op jit(solution)/shard_map/ppermute | solution.py:10
  171.4 259.4 %all-reduce.2.cloned.1.call-done = f32[2048,384]{1,0:T(8,128)} async-done(((f32[2048,384]{1,0:T(8,128)}), f32[2048,384]{1,0:T(8,128)}) %all-reduce.2.cloned.1.call-update) | async-done | bytes 3145744 | tf_op jit(solution)/shard_map/psum | solution.py:86
  430.8 0.8 multiply_reduce_fusion.9
  432.2 1.4 divide_subtract_fusion.6
  (109 shorter events, 18.4 us)
Async XLA Ops:
  7.2 6.2 %copy-start.1 = (f32[1,1,128,384]{3,2,1,0:T(8,128)S(1)}, f32[1,1,128,384]{3,2,1,0:T(8,128)}, u32[]{:S(2)}) copy-start(f32[1,1,128,384]{3,2,1,0:T(8,128)} %param.17) | copy-start | bytes 589828
  7.2 6.2 %copy-start = (f32[1,1,128,384]{3,2,1,0:T(8,128)S(1)}, f32[1,1,128,384]{3,2,1,0:T(8,128)}, u32[]{:S(2)}) copy-start(f32[1,1,128,384]{3,2,1,0:T(8,128)} %param.19) | copy-start | bytes 589828
  7.2 423.6 %all-reduce.2.cloned.1.call-start = ((), (), s32[]{:S(2)}) async-start(), calls=%async_computation | async-start | bytes 6291456 | tf_op jit(solution)/shard_map/psum | solution.py:86
  13.4 16.8 %copy-start.2 = (f32[1,1,128]{2,1,0:T(1,128)S(1)}, f32[1,1,128]{2,1,0:T(1,128)}, u32[]{:S(2)}) copy-start(f32[1,1,128]{2,1,0:T(1,128)} %param.18) | copy-start | bytes 1540
  13.4 19.0 %copy-start.3 = (f32[1,1,128]{2,1,0:T(1,128)S(1)}, f32[1,1,128]{2,1,0:T(1,128)}, u32[]{:S(2)}) copy-start(f32[1,1,128]{2,1,0:T(1,128)} %param.20) | copy-start | bytes 1540
  30.3 30.8 %collective-permute-start = (f32[128,384]{1,0:T(8,128)S(1)}, f32[128,384]{1,0:T(8,128)S(1)}, u32[]{:S(2)}, u32[]{:S(2)}) collective-permute-start(f32[128,384]{1,0:T(8,128)S(1)} %divide_subtract_fusion.5), channel_id=1, source_target_pairs={{480,0},{0,32},{32,64},{64,96},{96,128},{128,160},{160,192},{192,2... | collective-permute-start | bytes 589832 | tf_op jit(solution)/shard_map/ppermute | solution.py:10
  32.5 36.4 %collective-permute-start.1 = (f32[128,384]{1,0:T(8,128)S(1)}, f32[128,384]{1,0:T(8,128)S(1)}, u32[]{:S(2)}, u32[]{:S(2)}) collective-permute-start(f32[128,384]{1,0:T(8,128)S(1)} %divide_subtract_fusion.4), channel_id=1, source_target_pairs={{31,0},{0,1},{1,2},{2,3},{3,4},{4,5},{5,6},{6,7},{7,8},{8,9},{9,10... | collective-permute-start | bytes 589832 | tf_op jit(solution)/shard_map/ppermute | solution.py:10
  36.0 49.8 %collective-permute-start.2 = (f32[128]{0:T(128)S(1)}, f32[128]{0:T(128)S(1)}, u32[]{:S(2)}, u32[]{:S(2)}) collective-permute-start(f32[128]{0:T(128)S(1)} %get-tuple-element.301), channel_id=1, source_target_pairs={{480,0},{0,32},{32,64},{64,96},{96,128},{128,160},{160,192},{192,2... | collective-permute-start | bytes 1544 | tf_op jit(solution)/shard_map/ppermute | solution.py:10
  42.6 45.3 %collective-permute-start.4 = (f32[128]{0:T(128)S(1)}, f32[128]{0:T(128)S(1)}, u32[]{:S(2)}, u32[]{:S(2)}) collective-permute-start(f32[128]{0:T(128)S(1)} %get-tuple-element.299), channel_id=1, source_target_pairs={{31,0},{0,1},{1,2},{2,3},{3,4},{4,5},{5,6},{6,7},{7,8},{8,9},{9,10... | collective-permute-start | bytes 1544 | tf_op jit(solution)/shard_map/ppermute | solution.py:10
  85.9 12.7 %collective-permute-start.3 = (f32[128,384]{1,0:T(8,128)S(1)}, f32[128,384]{1,0:T(8,128)S(1)}, u32[]{:S(2)}, u32[]{:S(2)}) collective-permute-start(f32[128,384]{1,0:T(8,128)S(1)} %divide_subtract_fusion.3), channel_id=1, source_target_pairs={{480,0},{0,32},{32,64},{64,96},{96,128},{128,160},{160,192},{192,2... | collective-permute-start | bytes 589832 | tf_op jit(solution)/shard_map/ppermute | solution.py:10
  88.0 24.5 %collective-permute-start.5 = (f32[128,384]{1,0:T(8,128)S(1)}, f32[128,384]{1,0:T(8,128)S(1)}, u32[]{:S(2)}, u32[]{:S(2)}) collective-permute-start(f32[128,384]{1,0:T(8,128)S(1)} %divide_subtract_fusion.2), channel_id=1, source_target_pairs={{31,0},{0,1},{1,2},{2,3},{3,4},{4,5},{5,6},{6,7},{7,8},{8,9},{9,10... | collective-permute-start | bytes 589832 | tf_op jit(solution)/shard_map/ppermute | solution.py:10
  145.5 286.2 %copy-start.4 = (f32[4]{0:T(128)S(1)}, f32[4]{0:T(128)}, u32[]{:S(2)}) copy-start(f32[4]{0:T(128)} %param.22) | copy-start | bytes 52
  145.5 4.9 %collective-permute-start.6 = (f32[128]{0:T(128)S(1)}, f32[128]{0:T(128)S(1)}, u32[]{:S(2)}, u32[]{:S(2)}) collective-permute-start(f32[128]{0:T(128)S(1)} %get-tuple-element.297), channel_id=1, source_target_pairs={{480,0},{0,32},{32,64},{64,96},{96,128},{128,160},{160,192},{192,2... | collective-permute-start | bytes 1544 | tf_op jit(solution)/shard_map/ppermute | solution.py:10
  147.5 9.3 %collective-permute-start.9 = (f32[128]{0:T(128)S(1)}, f32[128]{0:T(128)S(1)}, u32[]{:S(2)}, u32[]{:S(2)}) collective-permute-start(f32[128]{0:T(128)S(1)} %get-tuple-element.295), channel_id=1, source_target_pairs={{31,0},{0,1},{1,2},{2,3},{3,4},{4,5},{5,6},{6,7},{7,8},{8,9},{9,10... | collective-permute-start | bytes 1544 | tf_op jit(solution)/shard_map/ppermute | solution.py:10
  150.5 20.9 %collective-permute-start.7 = (f32[128,384]{1,0:T(8,128)S(1)}, f32[128,384]{1,0:T(8,128)S(1)}, u32[]{:S(2)}, u32[]{:S(2)}) collective-permute-start(f32[128,384]{1,0:T(8,128)S(1)} %divide_subtract_fusion.1), channel_id=1, source_target_pairs={{480,0},{0,32},{32,64},{64,96},{96,128},{128,160},{160,192},{192,2... | collective-permute-start | bytes 589832 | tf_op jit(solution)/shard_map/ppermute | solution.py:10
  156.9 14.5 %collective-permute-start.10 = (f32[128,384]{1,0:T(8,128)S(1)}, f32[128,384]{1,0:T(8,128)S(1)}, u32[]{:S(2)}, u32[]{:S(2)}) collective-permute-start(f32[128,384]{1,0:T(8,128)S(1)} %divide_subtract_fusion), channel_id=1, source_target_pairs={{31,0},{0,1},{1,2},{2,3},{3,4},{4,5},{5,6},{6,7},{7,8},{8,9},{9,10... | collective-permute-start | bytes 589832 | tf_op jit(solution)/shard_map/ppermute | solution.py:10
  158.8 4.9 %collective-permute-start.8 = (f32[128]{0:T(128)S(1)}, f32[128]{0:T(128)S(1)}, u32[]{:S(2)}, u32[]{:S(2)}) collective-permute-start(f32[128]{0:T(128)S(1)} %get-tuple-element.293), channel_id=1, source_target_pairs={{480,0},{0,32},{32,64},{64,96},{96,128},{128,160},{160,192},{192,2... | collective-permute-start | bytes 1544 | tf_op jit(solution)/shard_map/ppermute | solution.py:10
  160.8 10.6 %collective-permute-start.11 = (f32[128]{0:T(128)S(1)}, f32[128]{0:T(128)S(1)}, u32[]{:S(2)}, u32[]{:S(2)}) collective-permute-start(f32[128]{0:T(128)S(1)} %get-tuple-element.291), channel_id=1, source_target_pairs={{31,0},{0,1},{1,2},{2,3},{3,4},{4,5},{5,6},{6,7},{7,8},{8,9},{9,10... | collective-permute-start | bytes 1544 | tf_op jit(solution)/shard_map/ppermute | solution.py:10
Sparse Core Ops, SparseCore 0:
  145.6 285.1 all-reduce.1
where the time goes:
time: 446 us; the launch traced here: 443 us
  waiting for transfers between devices  295 us (66%)
  starting transfers between devices  54.6 us (12%)
  other arithmetic  42.5 us (10%)
  local copies, waits for them, and re-layouts  28.8 us (6%)
  between operations  14.4 us (3%)
  loops' own time  5.13 us (1%)
    psum x1, waiting for transfers between devices, on_device(): total = lax.psum(grad_rel, ('src', 'dst'))  259 us
    ppermute x12, starting transfers between devices, shifted(): return lax.ppermute(block, axis, route)  54.5 us
    ppermute x12, waiting for transfers between devices, shifted(): return lax.ppermute(block, axis, route)  35.6 us
    scatter-add x4, other arithmetic, group_terms(): grad_rel = grad_rel.at[r_idx].add(grad_prod * src_vec)  19.6 us
    scatter-add x8, other arithmetic, group_terms(): grad_dst.at[d_idx].add(grad_pos[:, None] * product).at[n_idx]  11.9 us
    gather x4, local copies, waits for them, and re-layouts, group_terms(): rel_vec = relations[r_idx]  10.9 us
  transfers between devices with their start and end apart: 13, of which 7 were waited for; matrix products, arithmetic and copies ran while one was open for 4% of the time, Pallas kernels for 0%

commit v1 on v0

--- a/solution.py
+++ b/solution.py
@@ -1,7 +1,14 @@
 import jax
 import jax.numpy as jnp
 from jax import lax
+from jax.experimental import pallas as pl
+from jax.experimental.pallas import tpu as pltpu
 from jax.sharding import PartitionSpec as P
+
+MESH = pl.DeviceIdType.MESH
+ORDERS = (("z", "y", "x"), ("y", "x", "z"), ("x", "z", "y"))
+SIZE = {"x": 4, "y": 8, "z": 8}
+ROUND = ((2, 0), (0, 0), (1, 0), (2, 1), (0, 1), (1, 1), (2, 2), (0, 2), (1, 2))
 
 
 def shifted(block, axis, distance):
@@ -44,6 +51,143 @@
     grad_dst = grad_dst.at[d_idx].add(grad_pos[:, None] * product).at[n_idx].add(grad_negrows)
     grad_rel = grad_rel.at[r_idx].add(grad_prod * src_vec)
     return (grad_src, grad_dst, grad_rel)
+
+
+def coords():
+    s, d = lax.axis_index("src"), lax.axis_index("dst")
+    return {
+        "core": lax.rem(s, 2),
+        "x": lax.rem(lax.div(s, 2), 4),
+        "y": lax.div(s, 8) * 4 + lax.rem(d, 4),
+        "z": lax.div(d, 4),
+    }
+
+
+def device_of(at):
+    return (
+        lax.div(at["y"], 4) * 8 + at["x"] * 2 + at["core"],
+        at["z"] * 4 + lax.rem(at["y"], 4),
+    )
+
+
+def partner(me, axis, offset):
+    return device_of({**me, axis: lax.rem(me[axis] + offset, SIZE[axis])})
+
+
+def sum_kernel(g_ref, out_ref, core_in, *rest):
+    half = rest[0]
+    recv = {(c, p): rest[1 + c * 3 + p] for c in range(3) for p in range(3)}
+    held = {(c, p): rest[10 + c * 2 + p] for c in range(3) for p in range(2)}
+    core_sem, send_sem, recv_sem = rest[16:]
+    me = coords()
+    sibling = device_of({**me, "core": 1 - me["core"]})
+    barrier = pltpu.get_barrier_semaphore()
+    pl.semaphore_signal(barrier, inc=1, device_id=sibling, device_id_type=MESH)
+    for axis in "xyz":
+
+        @pl.loop(1, SIZE[axis])
+        def _(o):
+            pl.semaphore_signal(
+                barrier, inc=1, device_id=partner(me, axis, o), device_id_type=MESH
+            )
+
+    pl.semaphore_wait(barrier, 18)
+
+    def core_copy(c):
+        return pltpu.make_async_remote_copy(
+            g_ref.at[c, 1 - me["core"]],
+            core_in.at[c],
+            core_sem.at[0, c],
+            core_sem.at[1, c],
+            device_id=sibling,
+            device_id_type=MESH,
+        )
+
+    def rows_of(c, p, j):
+        if p == 2:
+            return pl.ds(pl.multiple_of(lax.div(j, 2) * 8, 8), 8)
+        count = recv[c, p].shape[1]
+        return pl.ds(pl.multiple_of(j * count, count), count)
+
+    def start_phase(c, p):
+        axis = ORDERS[c][p]
+        source = half.at[c] if p == 0 else held[c, p - 1]
+
+        @pl.loop(1, SIZE[axis])
+        def _(o):
+            target = lax.rem(me[axis] + o, SIZE[axis])
+            pltpu.make_async_remote_copy(
+                source.at[rows_of(c, p, target)],
+                recv[c, p].at[o - 1],
+                send_sem.at[c, p],
+                recv_sem.at[c, p],
+                device_id=partner(me, axis, o),
+                device_id_type=MESH,
+            ).start()
+
+    def finish_phase(c, p):
+        axis = ORDERS[c][p]
+        pltpu.make_async_remote_copy(
+            recv[c, p],
+            recv[c, p],
+            send_sem.at[c, p],
+            recv_sem.at[c, p],
+            device_id=sibling,
+            device_id_type=MESH,
+        ).wait()
+        source = half.at[c] if p == 0 else held[c, p - 1]
+        total = source[rows_of(c, p, me[axis]), :]
+        for o in range(SIZE[axis] - 1):
+            total = total + recv[c, p][o]
+        return total
+
+    for c in (2, 0, 1):
+        core_copy(c).start()
+    for c in (2, 0, 1):
+        core_copy(c).wait()
+        half[c] = g_ref[c, me["core"]] + core_in[c]
+        start_phase(c, 0)
+    for c, p in ROUND:
+        total = finish_phase(c, p)
+        if p < 2:
+            held[c, p][...] = total
+            start_phase(c, p + 1)
+        else:
+            odd = lax.rem(me[ORDERS[c][2]], 2)
+            out_ref[:, c * 128 : (c + 1) * 128] = jnp.where(odd == 0, total[0:4], total[4:8])
+
+
+def relation_total(grad_rel):
+    g = grad_rel.reshape(2, 4, 2, 8, 4, 4, 3, 128)
+    thirds = (
+        g[..., 0, :].transpose(2, 3, 0, 4, 1, 5, 6),
+        g[..., 1, :].transpose(2, 0, 4, 1, 3, 5, 6),
+        g[..., 2, :].transpose(2, 1, 3, 0, 4, 5, 6),
+    )
+    g = jnp.stack([t.reshape(2, 1024, 128) for t in thirds])
+    chunk = ((128, 16, 8), (128, 32, 8), (256, 32, 8))
+    scratch = [pltpu.VMEM((3, 1024, 128), jnp.float32), pltpu.VMEM((3, 1024, 128), jnp.float32)]
+    for c in range(3):
+        for p in range(3):
+            scratch.append(pltpu.VMEM((SIZE[ORDERS[c][p]] - 1, chunk[c][p], 128), jnp.float32))
+    for c in range(3):
+        for p in range(2):
+            scratch.append(pltpu.VMEM((chunk[c][p], 128), jnp.float32))
+    scratch += [
+        pltpu.SemaphoreType.DMA((2, 3)),
+        pltpu.SemaphoreType.DMA((3, 3)),
+        pltpu.SemaphoreType.DMA((3, 3)),
+    ]
+    return pl.pallas_call(
+        sum_kernel,
+        out_shape=jax.ShapeDtypeStruct((4, 384), jnp.float32),
+        in_specs=[pl.BlockSpec(memory_space=pltpu.VMEM)],
+        out_specs=pl.BlockSpec(memory_space=pltpu.VMEM),
+        scratch_shapes=scratch,
+        compiler_params=pltpu.CompilerParams(
+            collective_id=0, has_side_effects=True, vmem_limit_bytes=32 * 2**20
+        ),
+    )(g)
 
 
 def on_device(
@@ -83,8 +227,7 @@
         dst_blk, dst_st = shifted((dst_blk, dst_st), "dst", 1)
     share = rel_state.shape[0]
     first = lax.axis_index(("src", "dst")) * share
-    total = lax.psum(grad_rel, ("src", "dst"))
-    own_grad = lax.dynamic_slice_in_dim(total, first, share, 0)
+    own_grad = relation_total(grad_rel)
     own_rel = lax.dynamic_slice_in_dim(relations, first, share, 0)
     updated_relation, updated_relation_state = adagrad_update(own_rel, rel_state, own_grad)
     return (

time: 446 us -> 214 us (0.48)
  waiting for transfers between devices: 295 us -> 13.6 us
  Pallas kernels: 0 us -> 43.1 us
  local copies, waits for them, and re-layouts: 28.8 us -> 48.7 us
  between operations: 14.4 us -> 1.06 us
  other arithmetic: 42.5 us -> 51.6 us
  starting transfers between devices: 54.6 us -> 45.9 us
    psum x1 -> x0, waiting for transfers between devices: 259 us -> none  [on_device(): total = lax.psum(grad_rel, ('src', 'dst'))]
    pallas_call x0 -> x1, Pallas kernels: none -> 43.1 us  [relation_total(): pl.pallas_call(sum_kernel, out_shape=jax.ShapeDtypeStruct((4, 384), jnp.f...]
    ppermute x12, waiting for transfers between devices: 35.6 us -> 13.6 us  [shifted(): return lax.ppermute(block, axis, route)]
    ppermute x12, starting transfers between devices: 54.5 us -> 45.9 us  [shifted(): return lax.ppermute(block, axis, route)]
    slice x0 -> x1, local copies, waits for them, and re-layouts: none -> 8.53 us  [relation_total(): g[..., 0, :].transpose(2, 3, 0, 4, 1, 5, 6)]
    reshape x0 -> x1, local copies, waits for them, and re-layouts: none -> 5.76 us  [relation_total(): g = grad_rel.reshape(2, 4, 2, 8, 4, 4, 3, 128)]
    scatter-add x4 -> x5, other arithmetic: 19.6 us -> 24.4 us  [group_terms(): grad_rel = grad_rel.at[r_idx].add(grad_prod * src_vec)]
    scatter-add x8 -> x10, other arithmetic: 11.9 us -> 14.9 us  [group_terms(): grad_dst.at[d_idx].add(grad_pos[:, None] * product).at[n_idx]]
  transfers between devices with their start and end apart: 13 -> 12, of which waited for: 7 -> 2; matrix products, arithmetic and copies ran while one was open for 4% -> 37% of each run, Pallas kernels for 0% -> 20%
where the time goes in v1:
time: 214 us; the launch traced here: 213 us
  other arithmetic  51.6 us (24%)
  local copies, waits for them, and re-layouts  48.7 us (23%)
  starting transfers between devices  45.9 us (21%)
  Pallas kernels  43.1 us (20%)
  waiting for transfers between devices  13.6 us (6%)
  loops' own time  5.88 us (3%)
  matrix products  2.94 us (1%)
    ppermute x12, starting transfers between devices, shifted(): return lax.ppermute(block, axis, route)  45.9 us
    pallas_call x1, Pallas kernels, relation_total(): pl.pallas_call(sum_kernel, out_shape=jax.ShapeDtypeStruct((4, 384), jnp.f...  43.1 us
    scatter-add x5, other arithmetic, group_terms(): grad_rel = grad_rel.at[r_idx].add(grad_prod * src_vec)  24.4 us
    scatter-add x10, other arithmetic, group_terms(): grad_dst.at[d_idx].add(grad_pos[:, None] * product).at[n_idx]  14.9 us
    gather x5, local copies, waits for them, and re-layouts, group_terms(): rel_vec = relations[r_idx]  13.7 us
    ppermute x12, waiting for transfers between devices, shifted(): return lax.ppermute(block, axis, route)  13.6 us
    slice x1, local copies, waits for them, and re-layouts, relation_total(): g[..., 0, :].transpose(2, 3, 0, 4, 1, 5, 6)  8.53 us
    scatter-add x5, other arithmetic, group_terms(): grad_src = grad_src.at[s_idx].add(grad_prod * rel_vec)  7.33 us
  transfers between devices with their start and end apart: 12, of which 2 were waited for; matrix products, arithmetic and copies ran while one was open for 37% of the time, Pallas kernels for 20%

profile of v1, /device:TPU:6, one launch (start us, length us, event | category | flops | bytes accessed | tf_op | source)
XLA Modules:
  0.0 212.9 jit_solution(1735103816714459635)
XLA Ops:
  0.7 1.4 fusion.65
  4.9 1.9 broadcast_in_dim.51
  6.8 16.7 %while.42 = (s32[]{:T(128)}, f32[128,384]{1,0:T(8,128)S(1)}, f32[128,384]{1,0:T(8,128)S(1)}, f32[2048,384]{1,0:T(8,128)}, s32[]{:T(128)}, /*index=5*/s32[256]{0:...) while((s32[]{:T(128)}, f32[128,384]{1,0:T(8,128)S(1)}, ...), condition=%wide.region_6.7_spmd, body=%wide.region_0.6_spmd.sunk | while | flops 38524680 | bytes 8580353 | solution.py:221
  10.0 2.7 %gather_fusion.3 = f32[128,384]{1,0:T(8,128)S(1)} fusion(f32[2048,384]{1,0:T(8,128)} %get-tuple-element.614, s32[1024]{0:T(1024)S(1)} %pad_clamp_fusion.27), kind=kCustom, calls=%fused_computation.1.clone.1 | custom fusion | bytes 393728 | tf_op jit(solution)/shard_map/while/body/gather | solution.py:34
  13.3 1.5 scatter_custom_fusion.45
  14.7 1.5 scatter_custom_fusion.46
  16.5 1.4 scatter_fusion
  17.9 4.9 %scatter_custom_fusion.48 = f32[2048,384]{1,0:T(8,128)} fusion(f32[2048,384]{1,0:T(8,128)} %get-tuple-element.592, s32[128]{0:T(128)S(1)} %get-tuple-element.537, f32[128,384]{1,0:T(8,128)S(1)} %convolution_add_fusion.6, f32[128,384]{1,0:T(8,128)S(1)} %gather_fusion.2), kind=kCustom, calls=%fused_computation.31.clone.1 | custom fusion | flops 98304 | bytes 3538944 | tf_op jit(solution)/shard_map/while/body/scatter-add | solution.py:52
  23.7 1.9 collective-permute-start
  25.9 19.3 %collective-permute-start.1 = (f32[128,384]{1,0:T(8,128)S(1)}, f32[128,384]{1,0:T(8,128)S(1)}, u32[]{:S(2)}, u32[]{:S(2)}) collective-permute-start(f32[128,384]{1,0:T(8,128)S(1)} %divide_subtract_fusion.4), channel_id=1, source_target_pairs={{31,0},{0,1},{1,2},{2,3},{3,4},{4,5},{5,6},{6,7},{7,8},{8,9},{9,10... | collective-permute-start | bytes 589832 | tf_op jit(solution)/shard_map/ppermute | solution.py:17
  45.2 6.4 %collective-permute-start.2 = (f32[128]{0:T(128)S(1)}, f32[128]{0:T(128)S(1)}, u32[]{:S(2)}, u32[]{:S(2)}) collective-permute-start(f32[128]{0:T(128)S(1)} %get-tuple-element.301), channel_id=1, source_target_pairs={{480,0},{0,32},{32,64},{64,96},{96,128},{128,160},{160,192},{192,2... | collective-permute-start | bytes 1544 | tf_op jit(solution)/shard_map/ppermute | solution.py:17
  51.5 3.0 %collective-permute-start.4 = (f32[128]{0:T(128)S(1)}, f32[128]{0:T(128)S(1)}, u32[]{:S(2)}, u32[]{:S(2)}) collective-permute-start(f32[128]{0:T(128)S(1)} %get-tuple-element.299), channel_id=1, source_target_pairs={{31,0},{0,1},{1,2},{2,3},{3,4},{4,5},{5,6},{6,7},{7,8},{8,9},{9,10... | collective-permute-start | bytes 1544 | tf_op jit(solution)/shard_map/ppermute | solution.py:17
  54.5 7.3 %collective-permute-done.1 = f32[128,384]{1,0:T(8,128)S(1)} collective-permute-done((f32[128,384]{1,0:T(8,128)S(1)}, f32[128,384]{1,0:T(8,128)S(1)}, u32[]{:S(2)}, u32[]{:S(2)}) %collective-permute-start.1) | collective-permute-done | bytes 196640 | tf_op jit(solution)/shard_map/ppermute | solution.py:17
  61.9 32.6 %while.43 = (s32[]{:T(128)}, f32[128,384]{1,0:T(8,128)S(1)}, f32[128,384]{1,0:T(8,128)S(1)}, f32[2048,384]{1,0:T(8,128)}, s32[]{:T(128)}, /*index=5*/s32[256]{0:...) while((s32[]{:T(128)}, f32[128,384]{1,0:T(8,128)S(1)}, ...), condition=%wide.region_15.16_spmd, body=%wide.region_9.15_spmd.sunk | while | flops 38524680 | bytes 8580353 | solution.py:221
  65.1 2.7 %gather_fusion.7 = f32[128,384]{1,0:T(8,128)S(1)} fusion(f32[2048,384]{1,0:T(8,128)} %get-tuple-element.665, s32[1024]{0:T(1024)S(1)} %pad_clamp_fusion.31), kind=kCustom, calls=%fused_computation.5.clone.1 | custom fusion | bytes 393728 | tf_op jit(solution)/shard_map/while/body/gather | solution.py:34
  68.3 1.5 scatter_custom_fusion.52
  69.8 1.5 scatter_custom_fusion.53
  71.5 1.4 scatter_fusion.1
  73.0 4.9 %scatter_custom_fusion.55 = f32[2048,384]{1,0:T(8,128)} fusion(f32[2048,384]{1,0:T(8,128)} %get-tuple-element.643, s32[128]{0:T(128)S(1)} %get-tuple-element.553, f32[128,384]{1,0:T(8,128)S(1)} %convolution_add_fusion.7, f32[128,384]{1,0:T(8,128)S(1)} %gather_fusion.6), kind=kCustom, calls=%fused_computation.61.clone.1 | custom fusion | flops 98304 | bytes 3538944 | tf_op jit(solution)/shard_map/while/body/scatter-add | solution.py:52
  81.1 2.7 %gather_fusion.7 = f32[128,384]{1,0:T(8,128)S(1)} fusion(f32[2048,384]{1,0:T(8,128)} %get-tuple-element.665, s32[1024]{0:T(1024)S(1)} %pad_clamp_fusion.31), kind=kCustom, calls=%fused_computation.5.clone.1 | custom fusion | bytes 393728 | tf_op jit(solution)/shard_map/while/body/gather | solution.py:34
  84.3 1.5 scatter_custom_fusion.52
  85.8 1.5 scatter_custom_fusion.53
  87.5 1.4 scatter_fusion.1
  89.0 4.9 %scatter_custom_fusion.55 = f32[2048,384]{1,0:T(8,128)} fusion(f32[2048,384]{1,0:T(8,128)} %get-tuple-element.643, s32[128]{0:T(128)S(1)} %get-tuple-element.553, f32[128,384]{1,0:T(8,128)S(1)} %convolution_add_fusion.7, f32[128,384]{1,0:T(8,128)S(1)} %gather_fusion.6), kind=kCustom, calls=%fused_computation.61.clone.1 | custom fusion | flops 98304 | bytes 3538944 | tf_op jit(solution)/shard_map/while/body/scatter-add | solution.py:52
  94.7 1.9 collective-permute-start.3
  96.9 1.9 collective-permute-start.5
  98.8 1.9 collective-permute-start.6
  100.8 1.9 collective-permute-start.9
  102.7 6.3 %collective-permute-done.5 = f32[128,384]{1,0:T(8,128)S(1)} collective-permute-done((f32[128,384]{1,0:T(8,128)S(1)}, f32[128,384]{1,0:T(8,128)S(1)}, u32[]{:S(2)}, u32[]{:S(2)}) %collective-permute-start.5) | collective-permute-done | bytes 196640 | tf_op jit(solution)/shard_map/ppermute | solution.py:17
  109.0 32.8 %while.44 = (s32[]{:T(128)}, f32[128,384]{1,0:T(8,128)S(1)}, f32[128,384]{1,0:T(8,128)S(1)}, f32[2048,384]{1,0:T(8,128)}, s32[]{:T(128)}, /*index=5*/s32[256]{0:...) while((s32[]{:T(128)}, f32[128,384]{1,0:T(8,128)S(1)}, ...), condition=%wide.region_24.25_spmd, body=%wide.region_18.24_spmd.sunk | while | flops 38524680 | bytes 8580353 | solution.py:221
  112.4 2.7 %gather_fusion.11 = f32[128,384]{1,0:T(8,128)S(1)} fusion(f32[2048,384]{1,0:T(8,128)} %get-tuple-element.716, s32[1024]{0:T(1024)S(1)} %pad_clamp_fusion.35), kind=kCustom, calls=%fused_computation.9.clone.1 | custom fusion | bytes 393728 | tf_op jit(solution)/shard_map/while/body/gather | solution.py:34
  115.7 1.5 scatter_custom_fusion.59
  117.1 1.5 scatter_custom_fusion.60
  118.9 1.4 scatter_fusion.2
  120.3 4.9 %scatter_custom_fusion.62 = f32[2048,384]{1,0:T(8,128)} fusion(f32[2048,384]{1,0:T(8,128)} %get-tuple-element.694, s32[128]{0:T(128)S(1)} %get-tuple-element.569, f32[128,384]{1,0:T(8,128)S(1)} %convolution_add_fusion.8, f32[128,384]{1,0:T(8,128)S(1)} %gather_fusion.10), kind=kCustom, calls=%fused_computation.91.clone.1 | custom fusion | flops 98304 | bytes 3538944 | tf_op jit(solution)/shard_map/while/body/scatter-add | solution.py:52
  128.4 2.7 %gather_fusion.11 = f32[128,384]{1,0:T(8,128)S(1)} fusion(f32[2048,384]{1,0:T(8,128)} %get-tuple-element.716, s32[1024]{0:T(1024)S(1)} %pad_clamp_fusion.35), kind=kCustom, calls=%fused_computation.9.clone.1 | custom fusion | bytes 393728 | tf_op jit(solution)/shard_map/while/body/gather | solution.py:34
  131.6 1.5 scatter_custom_fusion.59
  133.1 1.5 scatter_custom_fusion.60
  134.9 1.4 scatter_fusion.2
  136.3 4.9 %scatter_custom_fusion.62 = f32[2048,384]{1,0:T(8,128)} fusion(f32[2048,384]{1,0:T(8,128)} %get-tuple-element.694, s32[128]{0:T(128)S(1)} %get-tuple-element.569, f32[128,384]{1,0:T(8,128)S(1)} %convolution_add_fusion.8, f32[128,384]{1,0:T(8,128)S(1)} %gather_fusion.10), kind=kCustom, calls=%fused_computation.91.clone.1 | custom fusion | flops 98304 | bytes 3538944 | tf_op jit(solution)/shard_map/while/body/scatter-add | solution.py:52
  142.1 1.9 collective-permute-start.7
  144.0 1.9 collective-permute-start.8
  146.2 1.9 collective-permute-start.10
  148.1 1.9 collective-permute-start.11
  150.0 5.8 %reshape.140 = f32[2,4,2,8,4,4,3,128]{7,6,5,4,3,2,1,0:T(4,128)} reshape(f32[2048,384]{1,0:T(8,128)} %get-tuple-element.209) | data formatting | bytes 6291456 | tf_op jit(solution)/shard_map/reshape | solution.py:161
  155.8 8.5 %fusion.61 = (f32[2,4,2,8,4,4,1,128]{7,6,5,4,3,2,1,0:T(1,128)S(1)}, f32[2,4,2,8,4,4,1,128]{7,6,5,4,3,2,1,0:T(1,128)S(1)}, f32[2,4,2,8,4,4,1,128]{7,6,5,4,3,2,1,0:T(1,128)S(1)}) fusion(f32[2,4,2,8,4,4,3,128]{7,6,5,4,3,2,1,0:T(4,128)} %reshape.140), kind=kLoop, calls=%fused_computation.146 | loop fusion | bytes 6291456 | tf_op jit(solution)/shard_map/slice | solution.py:163
  165.3 43.1 %shard_map.154 = f32[4,384]{1,0:T(4,128)S(1)} custom-call(f32[3,2,1024,128]{3,2,1,0:T(8,128)S(1)} %pad_maximum_fusion.g_ref), custom_call_target="tpu_custom_call" | custom-call | tf_op jit(solution)/shard_map/pallas_call | solution.py:181
  209.1 1.4 divide_subtract_fusion.6
  (133 shorter events, 24.2 us)
Async XLA Ops:
  0.6 6.2 %copy-start.1 = (f32[1,1,128,384]{3,2,1,0:T(8,128)S(1)}, f32[1,1,128,384]{3,2,1,0:T(8,128)}, u32[]{:S(2)}) copy-start(f32[1,1,128,384]{3,2,1,0:T(8,128)} %param.17) | copy-start | bytes 589828
  0.6 6.1 %copy-start = (f32[1,1,128,384]{3,2,1,0:T(8,128)S(1)}, f32[1,1,128,384]{3,2,1,0:T(8,128)}, u32[]{:S(2)}) copy-start(f32[1,1,128,384]{3,2,1,0:T(8,128)} %param.19) | copy-start | bytes 589828
  6.8 16.8 %copy-start.2 = (f32[1,1,128]{2,1,0:T(1,128)S(1)}, f32[1,1,128]{2,1,0:T(1,128)}, u32[]{:S(2)}) copy-start(f32[1,1,128]{2,1,0:T(1,128)} %param.18) | copy-start | bytes 1540
  6.8 18.9 %copy-start.3 = (f32[1,1,128]{2,1,0:T(1,128)S(1)}, f32[1,1,128]{2,1,0:T(1,128)}, u32[]{:S(2)}) copy-start(f32[1,1,128]{2,1,0:T(1,128)} %param.20) | copy-start | bytes 1540
  23.7 30.8 %collective-permute-start = (f32[128,384]{1,0:T(8,128)S(1)}, f32[128,384]{1,0:T(8,128)S(1)}, u32[]{:S(2)}, u32[]{:S(2)}) collective-permute-start(f32[128,384]{1,0:T(8,128)S(1)} %divide_subtract_fusion.5), channel_id=1, source_target_pairs={{480,0},{0,32},{32,64},{64,96},{96,128},{128,160},{160,192},{192,2... | collective-permute-start | bytes 589832 | tf_op jit(solution)/shard_map/ppermute | solution.py:17
  25.9 36.0 %collective-permute-start.1 = (f32[128,384]{1,0:T(8,128)S(1)}, f32[128,384]{1,0:T(8,128)S(1)}, u32[]{:S(2)}, u32[]{:S(2)}) collective-permute-start(f32[128,384]{1,0:T(8,128)S(1)} %divide_subtract_fusion.4), channel_id=1, source_target_pairs={{31,0},{0,1},{1,2},{2,3},{3,4},{4,5},{5,6},{6,7},{7,8},{8,9},{9,10... | collective-permute-start | bytes 589832 | tf_op jit(solution)/shard_map/ppermute | solution.py:17
  45.2 49.5 %collective-permute-start.2 = (f32[128]{0:T(128)S(1)}, f32[128]{0:T(128)S(1)}, u32[]{:S(2)}, u32[]{:S(2)}) collective-permute-start(f32[128]{0:T(128)S(1)} %get-tuple-element.301), channel_id=1, source_target_pairs={{480,0},{0,32},{32,64},{64,96},{96,128},{128,160},{160,192},{192,2... | collective-permute-start | bytes 1544 | tf_op jit(solution)/shard_map/ppermute | solution.py:17
  51.5 45.3 %collective-permute-start.4 = (f32[128]{0:T(128)S(1)}, f32[128]{0:T(128)S(1)}, u32[]{:S(2)}, u32[]{:S(2)}) collective-permute-start(f32[128]{0:T(128)S(1)} %get-tuple-element.299), channel_id=1, source_target_pairs={{31,0},{0,1},{1,2},{2,3},{3,4},{4,5},{5,6},{6,7},{7,8},{8,9},{9,10... | collective-permute-start | bytes 1544 | tf_op jit(solution)/shard_map/ppermute | solution.py:17
  94.7 8.0 %collective-permute-start.3 = (f32[128,384]{1,0:T(8,128)S(1)}, f32[128,384]{1,0:T(8,128)S(1)}, u32[]{:S(2)}, u32[]{:S(2)}) collective-permute-start(f32[128,384]{1,0:T(8,128)S(1)} %divide_subtract_fusion.3), channel_id=1, source_target_pairs={{480,0},{0,32},{32,64},{64,96},{96,128},{128,160},{160,192},{192,2... | collective-permute-start | bytes 589832 | tf_op jit(solution)/shard_map/ppermute | solution.py:17
  96.9 12.1 %collective-permute-start.5 = (f32[128,384]{1,0:T(8,128)S(1)}, f32[128,384]{1,0:T(8,128)S(1)}, u32[]{:S(2)}, u32[]{:S(2)}) collective-permute-start(f32[128,384]{1,0:T(8,128)S(1)} %divide_subtract_fusion.2), channel_id=1, source_target_pairs={{31,0},{0,1},{1,2},{2,3},{3,4},{4,5},{5,6},{6,7},{7,8},{8,9},{9,10... | collective-permute-start | bytes 589832 | tf_op jit(solution)/shard_map/ppermute | solution.py:17
  98.8 43.1 %collective-permute-start.6 = (f32[128]{0:T(128)S(1)}, f32[128]{0:T(128)S(1)}, u32[]{:S(2)}, u32[]{:S(2)}) collective-permute-start(f32[128]{0:T(128)S(1)} %get-tuple-element.297), channel_id=1, source_target_pairs={{480,0},{0,32},{32,64},{64,96},{96,128},{128,160},{160,192},{192,2... | collective-permute-start | bytes 1544 | tf_op jit(solution)/shard_map/ppermute | solution.py:17
  100.8 45.3 %collective-permute-start.9 = (f32[128]{0:T(128)S(1)}, f32[128]{0:T(128)S(1)}, u32[]{:S(2)}, u32[]{:S(2)}) collective-permute-start(f32[128]{0:T(128)S(1)} %get-tuple-element.295), channel_id=1, source_target_pairs={{31,0},{0,1},{1,2},{2,3},{3,4},{4,5},{5,6},{6,7},{7,8},{8,9},{9,10... | collective-permute-start | bytes 1544 | tf_op jit(solution)/shard_map/ppermute | solution.py:17
  142.1 68.4 %collective-permute-start.7 = (f32[128,384]{1,0:T(8,128)S(1)}, f32[128,384]{1,0:T(8,128)S(1)}, u32[]{:S(2)}, u32[]{:S(2)}) collective-permute-start(f32[128,384]{1,0:T(8,128)S(1)} %divide_subtract_fusion.1), channel_id=1, source_target_pairs={{480,0},{0,32},{32,64},{64,96},{96,128},{128,160},{160,192},{192,2... | collective-permute-start | bytes 589832 | tf_op jit(solution)/shard_map/ppermute | solution.py:17
  144.0 66.5 %collective-permute-start.8 = (f32[128]{0:T(128)S(1)}, f32[128]{0:T(128)S(1)}, u32[]{:S(2)}, u32[]{:S(2)}) collective-permute-start(f32[128]{0:T(128)S(1)} %get-tuple-element.293), channel_id=1, source_target_pairs={{480,0},{0,32},{32,64},{64,96},{96,128},{128,160},{160,192},{192,2... | collective-permute-start | bytes 1544 | tf_op jit(solution)/shard_map/ppermute | solution.py:17
  146.2 64.3 %collective-permute-start.10 = (f32[128,384]{1,0:T(8,128)S(1)}, f32[128,384]{1,0:T(8,128)S(1)}, u32[]{:S(2)}, u32[]{:S(2)}) collective-permute-start(f32[128,384]{1,0:T(8,128)S(1)} %divide_subtract_fusion), channel_id=1, source_target_pairs={{31,0},{0,1},{1,2},{2,3},{3,4},{4,5},{5,6},{6,7},{7,8},{8,9},{9,10... | collective-permute-start | bytes 589832 | tf_op jit(solution)/shard_map/ppermute | solution.py:17
  148.1 62.4 %collective-permute-start.11 = (f32[128]{0:T(128)S(1)}, f32[128]{0:T(128)S(1)}, u32[]{:S(2)}, u32[]{:S(2)}) collective-permute-start(f32[128]{0:T(128)S(1)} %get-tuple-element.291), channel_id=1, source_target_pairs={{31,0},{0,1},{1,2},{2,3},{3,4},{4,5},{5,6},{6,7},{7,8},{8,9},{9,10... | collective-permute-start | bytes 1544 | tf_op jit(solution)/shard_map/ppermute | solution.py:17
  165.3 43.3 %copy-start.4 = (f32[4]{0:T(128)S(1)}, f32[4]{0:T(128)}, u32[]{:S(2)}) copy-start(f32[4]{0:T(128)} %param.22) | copy-start | bytes 52

commit v2 on v1

v2 whole, which is shorter than its diff:
```python
import jax
import jax.numpy as jnp
from jax import lax
from jax.experimental import pallas as pl
from jax.experimental.pallas import tpu as pltpu
from jax.sharding import PartitionSpec as P

MESH = pl.DeviceIdType.MESH
F32, BF16, I32 = jnp.float32, jnp.bfloat16, jnp.int32
ORDERS = (("z", "y", "x"), ("y", "x", "z"), ("x", "z", "y"))
CHUNK = ((128, 16, 8), (128, 32, 8), (256, 32, 8))
SIZE = {"x": 4, "y": 8, "z": 8}
ROUND = ((2, 0), (0, 0), (1, 0), (2, 1), (0, 1), (1, 1), (2, 2), (0, 2), (1, 2))
STEPS = 3
EDGES_1, EDGES_2, NEXT, SRC_END, DST_END = (0, 31), (0, 30), (1, 31), (1, 2), (0, 3)


def coords():
    s, d = lax.axis_index("src"), lax.axis_index("dst")
    return {
        "core": lax.rem(s, 2),
        "x": lax.rem(lax.div(s, 2), 4),
        "y": lax.div(s, 8) * 4 + lax.rem(d, 4),
        "z": lax.div(d, 4),
    }


def device_of(at):
    return (
        lax.div(at["y"], 4) * 8 + at["x"] * 2 + at["core"],
        at["z"] * 4 + lax.rem(at["y"], 4),
    )


def partner(me, axis, offset):
    return device_of({**me, axis: lax.rem(me[axis] + offset, SIZE[axis])})


def moved(offset):
    s, d = lax.axis_index("src"), lax.axis_index("dst")
    return (lax.rem(s + offset[0], 16), lax.rem(d + offset[1], 32))


def dot(a, b):
    return jnp.dot(a, b, preferred_element_type=F32)


def dot_nt(a, b):
    return lax.dot_general(a, b, (((1,), (1,)), ((), ())), preferred_element_type=F32)


def one_hot(mask):
    return jnp.where(mask, 1.0, 0.0).astype(BF16)


def split(value, axis=0):
    high = value.astype(BF16)
    low = (value - high.astype(F32)).astype(BF16)
    return jnp.concatenate([high, low], axis=axis)


def sigmoid(value):
    return 1.0 / (1.0 + jnp.exp(-value))


def eye():
    return lax.broadcasted_iota(I32, (128, 128), 0) == lax.broadcasted_iota(I32, (128, 128), 1)


def as_column(row):
    return jnp.sum(jnp.where(eye(), row, 0.0), axis=1, keepdims=True)


def as_row(column):
    return jnp.sum(jnp.where(eye(), column, 0.0), axis=0, keepdims=True)


def adagrad(block, state_row, grad):
    state = as_column(state_row) + jnp.sum(grad * grad, axis=1, keepdims=True) * (1.0 / 384)
    return block - 0.1 * grad / jnp.sqrt(state), as_row(state)


def positions(r, c):
    k, z, x = r & 3, (r >> 4) & 7, (r >> 8) & 3
    y = ((r >> 10) << 2) | ((r >> 2) & 3)
    if c == 0:
        return (((z * 8 + y) * 4 + x) * 4) + k
    if c == 1:
        return (((y * 4 + x) * 8 + z) * 4) + k
    return (((x * 8 + z) * 8 + y) * 4) + k


def window_kernel(
    src_ref, src_st_ref, dst_ref, dst_st_ref, rel_hbm, rel_st_ref, idx_ref,
    src_out, src_st_out, dst_out, dst_st_out, rel_out, rel_st_out,
    table, idx, idx_sib, idx_smem, src_in, src_st_in, src_new, src_st_new, dst_cur, dst_st_cur,
    rel_vec, v_own, v_sib, half, *rest,
):
    recv = {(c, p): rest[c * 3 + p] for c in range(3) for p in range(3)}
    held = {(c, p): rest[9 + c * 2 + p] for c in range(3) for p in range(2)}
    (table_sem, smem_sem, idx_sem, sib_idx_sem, block_sem, state_sem, v_sem, end_sem,
     send_sem, recv_sem) = rest[15:]
    me = coords()
    sibling = device_of({**me, "core": 1 - me["core"]})

    load_table = pltpu.make_async_copy(rel_hbm, table, table_sem)
    load_table.start()

    barrier = pltpu.get_barrier_semaphore()
    pl.semaphore_signal(barrier, inc=1, device_id=sibling, device_id_type=MESH)
    for axis in "xyz":

        @pl.loop(1, SIZE[axis])
        def _(o):
            pl.semaphore_signal(
                barrier, inc=1, device_id=partner(me, axis, o), device_id_type=MESH
            )

    for ds, dd in (EDGES_1, EDGES_2, NEXT, SRC_END, DST_END):
        for offset in ((ds, dd), ((16 - ds) % 16, (32 - dd) % 32)):
            pl.semaphore_signal(barrier, inc=1, device_id=moved(offset), device_id_type=MESH)

    idx[0] = idx_ref[0]
    src_in[0] = src_ref[...]
    src_st_in[0] = src_st_ref[...]
    dst_cur[...] = dst_ref[...]
    dst_st_cur[...] = dst_st_ref[...]
    half[...] = jnp.zeros_like(half)
    pl.semaphore_wait(barrier, 28)

    def remote(source, target, sems, to):
        return pltpu.make_async_remote_copy(
            source, target, sems.at[0], sems.at[1], device_id=to, device_id_type=MESH
        )

    def edge_copy(t, offset):
        return remote(idx_ref.at[t], idx.at[t], idx_sem.at[t], moved(offset))

    def sib_idx_copy(t):
        return remote(idx.at[t], idx_sib.at[t], sib_idx_sem.at[t], sibling)

    def v_copy(t):
        return remote(v_own.at[t], v_sib.at[t], v_sem.at[t], sibling)

    def block_copy(t):
        return remote(src_new.at[t], src_in.at[t + 1], block_sem.at[t], moved(NEXT))

    def state_copy(t):
        return remote(src_st_new.at[t], src_st_in.at[t + 1], state_sem.at[t], moved(NEXT))

    edges = (None, edge_copy(1, EDGES_1), edge_copy(2, EDGES_2))
    edges[1].start()
    edges[2].start()
    sib_idx_copy(0).start()

    def gather_relations(t):
        load = pltpu.make_async_copy(idx.at[t], idx_smem.at[t], smem_sem)
        load.start()
        load.wait()

        @pl.loop(0, 32)
        def _(i):
            for j in range(8):
                e = i * 8 + j
                rel_vec[pl.ds(e, 1), :] = table[pl.ds(idx_smem[t, 2, e], 1), :]

    def add_third(t, c):
        v = jnp.concatenate(
            [v_own[t, :, c * 128 : (c + 1) * 128], v_sib[t, :, c * 128 : (c + 1) * 128]], axis=0
        )
        rhs = split(v, axis=1)
        r = jnp.concatenate([idx[t, 2:3, :], idx_sib[t, 2:3, :]], axis=1)
        at = jnp.where(((r >> 7) & 1) == me["core"], positions(r, c), -1)

        @pl.loop(0, 4)
        def _(ch):
            rows = pl.ds(pl.multiple_of(ch * 256, 256), 256)
            hot = one_hot(lax.broadcasted_iota(I32, (256, 512), 0) + ch * 256 == at)
            both = dot(hot, rhs)
            half[c, rows, :] += both[:, :128] + both[:, 128:]

    def work(t):
        rows = idx[t]
        columns = jnp.transpose(rows.astype(F32)).astype(I32)
        s_col, d_col, n_col = columns[:, 0:1], columns[:, 1:2], columns[:, 3:4]
        live = columns[:, 4:5].astype(F32)
        lanes = lax.broadcasted_iota(I32, (256, 256), 1) & 127
        src_blk, dst_blk = src_in[t], dst_cur[...]
        dst_two = split(dst_blk)
        src_vec = dot(one_hot(lanes == s_col), split(src_blk))
        dst_vec = dot(one_hot(lanes == d_col), dst_two)
        negb = dot(one_hot(lanes[:, :128] == n_col), dst_two[:128]).astype(BF16)
        rel = rel_vec[...]
        a = src_vec * rel
        ab = a.astype(BF16)
        pos = jnp.sum(a * dst_vec, axis=1, keepdims=True)
        gpos = -sigmoid(-pos) * live
        negs_part, rows_part = [], []
        for c in range(2):
            block = slice(c * 128, (c + 1) * 128)
            neg = dot_nt(ab[block], negb[block])
            gneg = sigmoid(neg) * (1.0 / 128) * live[block]
            negs_part.append(dot(gneg.astype(BF16), negb[block]))
            rows_part.append(dot(jnp.transpose(gneg).astype(BF16), ab[block]))
        gprod = gpos * dst_vec + jnp.concatenate(negs_part, axis=0)
        v_own[t] = gprod * src_vec
        v_copy(t).start()
        subl = lax.broadcasted_iota(I32, (128, 256), 0)
        s_hot = one_hot(subl == rows[0:1])
        grad_src = dot(jnp.concatenate([s_hot, s_hot], axis=1), split(gprod * rel))
        block, state = adagrad(src_blk, src_st_in[t], grad_src)
        src_new[t] = block
        src_st_new[t] = state

        @pl.when(t < 2)
        def _():
            state_copy(t).start()
            block_copy(t).start()

        d_hot = one_hot(subl == rows[1:2])
        n_hot = one_hot(subl == rows[3:4])
        grad_dst = dot(
            jnp.concatenate([d_hot, d_hot, n_hot, n_hot], axis=1),
            jnp.concatenate([split(gpos * a), split(jnp.concatenate(rows_part, axis=0))], axis=0),
        )
        block, state = adagrad(dst_blk, dst_st_cur[...], grad_dst)
        dst_cur[...] = block
        dst_st_cur[...] = state

    load_table.wait()

    @pl.loop(0, STEPS)
    def _(t):
        @pl.when(t > 0)
        def _():
            edge_copy(t, EDGES_1).wait()
            sib_idx_copy(t).start()

        gather_relations(t)

        @pl.when(t > 0)
        def _():
            sib_idx_copy(t - 1).wait()
            v_copy(t - 1).wait()
            for c in range(3):
                add_third(t - 1, c)
            state_copy(t - 1).wait()
            block_copy(t - 1).wait()

        work(t)

    ends = [
        remote(src_st_new.at[2], src_st_out, end_sem.at[0], moved(SRC_END)),
        remote(dst_st_cur, dst_st_out, end_sem.at[1], moved(DST_END)),
        remote(src_new.at[2], src_out, end_sem.at[2], moved(SRC_END)),
        remote(dst_cur, dst_out, end_sem.at[3], moved(DST_END)),
    ]

    def rows_of(c, p, j):
        if p == 2:
            return pl.ds(pl.multiple_of(lax.div(j, 2) * 8, 8), 8)
        return pl.ds(pl.multiple_of(j * CHUNK[c][p], CHUNK[c][p]), CHUNK[c][p])

    def start_phase(c, p):
        axis = ORDERS[c][p]
        source = half.at[c] if p == 0 else held[c, p - 1]

        @pl.loop(1, SIZE[axis])
        def _(o):
            target = lax.rem(me[axis] + o, SIZE[axis])
            pltpu.make_async_remote_copy(
                source.at[rows_of(c, p, target)],
                recv[c, p].at[o - 1],
                send_sem.at[c, p],
                recv_sem.at[c, p],
                device_id=partner(me, axis, o),
                device_id_type=MESH,
            ).start()

    def finish_phase(c, p):
        axis = ORDERS[c][p]
        pltpu.make_async_remote_copy(
            recv[c, p],
            recv[c, p],
            send_sem.at[c, p],
            recv_sem.at[c, p],
            device_id=sibling,
            device_id_type=MESH,
        ).wait()
        source = half.at[c] if p == 0 else held[c, p - 1]
        total = source[rows_of(c, p, me[axis]), :]
        for o in range(SIZE[axis] - 1):
            total = total + recv[c, p][o]
        return total

    sib_idx_copy(2).wait()
    v_copy(2).wait()
    for c in (2, 0, 1):
        add_third(2, c)
        start_phase(c, 0)
    for copy in ends:
        copy.start()
    last = {}
    for c, p in ROUND:
        total = finish_phase(c, p)
        if p < 2:
            held[c, p][...] = total
            start_phase(c, p + 1)
        else:
            odd = lax.rem(me[ORDERS[c][2]], 2)
            last[c] = jnp.where(odd == 0, total[0:4], total[4:8])
    grad = jnp.concatenate([last[0], last[1], last[2]], axis=1)
    owner = lax.axis_index("src") * 32 + lax.axis_index("dst")
    near = table[pl.ds(pl.multiple_of(lax.div(owner, 2) * 8, 8), 8), :]
    own = jnp.where(lax.rem(owner, 2) == 0, near[0:4], near[4:8])
    state = rel_st_ref[...] + jnp.sum(grad * grad, axis=1, keepdims=True) * (1.0 / 384)
    rel_st_out[...] = state
    rel_out[...] = own - 0.1 * grad / jnp.sqrt(state)
    for copy in ends:
        copy.wait()


def on_device(
    source_embedding_table,
    source_adagrad_state,
    destination_embedding_table,
    destination_adagrad_state,
    relations,
    rel_state,
    source_edge_rows,
    destination_edge_rows,
    edge_relation_index,
    negative_block_rows,
    bucket_block_counts,
):
    counts = bucket_block_counts[0, 0]
    live = (jnp.arange(256, dtype=I32)[None, :] // 128 < counts[:, None]).astype(I32)
    idx = jnp.stack(
        [
            source_edge_rows[0, 0],
            destination_edge_rows[0, 0],
            edge_relation_index[0, 0],
            negative_block_rows[0, 0].reshape(STEPS, 256),
            live,
            live,
            live,
            live,
        ],
        axis=1,
    )
    vmem = pl.BlockSpec(memory_space=pltpu.VMEM)
    dma = pltpu.SemaphoreType.DMA
    scratch = [
        pltpu.VMEM((2048, 384), F32),
        pltpu.VMEM((3, 8, 256), I32),
        pltpu.VMEM((3, 8, 256), I32),
        pltpu.SMEM((3, 8, 256), I32),
        pltpu.VMEM((3, 128, 384), F32),
        pltpu.VMEM((3, 1, 128), F32),
        pltpu.VMEM((3, 128, 384), F32),
        pltpu.VMEM((3, 1, 128), F32),
        pltpu.VMEM((128, 384), F32),
        pltpu.VMEM((1, 128), F32),
        pltpu.VMEM((256, 384), F32),
        pltpu.VMEM((3, 256, 384), F32),
        pltpu.VMEM((3, 256, 384), F32),
        pltpu.VMEM((3, 1024, 128), F32),
    ]
    for c in range(3):
        for p in range(3):
            scratch.append(pltpu.VMEM((SIZE[ORDERS[c][p]] - 1, CHUNK[c][p], 128), F32))
    for c in range(3):
        for p in range(2):
            scratch.append(pltpu.VMEM((CHUNK[c][p], 128), F32))
    scratch += [dma, dma, dma((3, 2)), dma((3, 2)), dma((2, 2)), dma((2, 2)), dma((3, 2)), dma((4, 2))]
    scratch += [dma((3, 3)), dma((3, 3))]
    block = jax.ShapeDtypeStruct((128, 384), F32)
    row = jax.ShapeDtypeStruct((1, 128), F32)
    src_out, src_st, dst_out, dst_st, rel_out, rel_st = pl.pallas_call(
        window_kernel,
        out_shape=(
            block,
            row,
            block,
            row,
            jax.ShapeDtypeStruct((4, 384), F32),
            jax.ShapeDtypeStruct((4, 1), F32),
        ),
        in_specs=[vmem, vmem, vmem, vmem, pl.BlockSpec(memory_space=pl.ANY), vmem, vmem],
        out_specs=(vmem,) * 6,
        scratch_shapes=scratch,
        compiler_params=pltpu.CompilerParams(
            collective_id=0, has_side_effects=True, vmem_limit_bytes=40 * 2**20
        ),
    )(
        source_embedding_table[0, 0],
        source_adagrad_state[0],
        destination_embedding_table[0, 0],
        destination_adagrad_state[0],
        relations,
        rel_state[:, None],
        idx,
    )
    return (
        src_out[None, None],
        src_st[None],
        dst_out[None, None],
        dst_st[None],
        rel_out,
        rel_st[:, 0],
    )


def solution(mesh):
    in_specs = (
        P("src", "dst", None, None),
        P("src", "dst", None),
        P("src", "dst", None, None),
        P("src", "dst", None),
        P(),
        P(("src", "dst")),
        P("src", "dst", None, None),
        P("src", "dst", None, None),
        P("src", "dst", None, None),
        P("src", "dst", None, None, None),
        P("src", "dst", None),
    )
    out_specs = (
        P("src", "dst", None, None),
        P("src", "dst", None),
        P("src", "dst", None, None),
        P("src", "dst", None),
        P(("src", "dst"), None),
        P(("src", "dst")),
    )
    return jax.shard_map(
        on_device, mesh=mesh, in_specs=in_specs, out_specs=out_specs, check_vma=False
    )
```

time: 214 us -> 87.5 us (0.41)
  the two profiles are of different devices: /device:TPU:6 before, /device:TPU:1 now
where the time goes in v2:
time: 87.5 us; the launch traced here: 87.2 us
  Pallas kernels  75.6 us (86%)
  local copies, waits for them, and re-layouts  9.53 us (11%)
  other arithmetic  1.36 us (2%)
    pallas_call x1, Pallas kernels, on_device(): pl.pallas_call(window_kernel, out_shape=(block, row, block, row, jax.Shap...  75.6 us
    unnamed x15, local copies, waits for them, and re-layouts  8.01 us

profile of v2, /device:TPU:1, one launch (start us, length us, event | category | flops | bytes accessed | tf_op | source)
XLA Modules:
  0.0 87.2 jit_solution(2336185325083108017)
XLA Ops:
  0.6 0.7 compare_convert_fusion
  1.4 0.7 copy.18.rel_st_ref
  2.1 0.8 stack.2.idx_ref
  2.9 0.0 copy-start
  2.9 1.9 %copy-done = f32[2048,384]{1,0:T(8,128)S(1)} copy-done((f32[2048,384]{1,0:T(8,128)S(1)}, f32[2048,384]{1,0:T(8,128)}, u32[]{:S(2)}) %copy-start) | copy-done | bytes 3145752
  4.8 0.0 copy-start.1
  4.8 0.9 %copy-done.1 = f32[1,1,128,384]{3,2,1,0:T(8,128)S(1)} copy-done((f32[1,1,128,384]{3,2,1,0:T(8,128)S(1)}, f32[1,1,128,384]{3,2,1,0:T(8,128)}, u32[]{:S(2)}) %copy-start.1) | copy-done | bytes 196632
  5.7 0.0 copy-start.2
  5.7 0.9 %copy-done.2 = f32[1,1,128,384]{3,2,1,0:T(8,128)S(1)} copy-done((f32[1,1,128,384]{3,2,1,0:T(8,128)S(1)}, f32[1,1,128,384]{3,2,1,0:T(8,128)}, u32[]{:S(2)}) %copy-start.2) | copy-done | bytes 196632
  6.6 0.0 copy-start.3
  6.6 0.7 copy-done.3
  7.3 0.0 copy-start.4
  7.3 0.7 copy-done.4
  8.0 75.6 %shard_map.154 = (f32[128,384]{1,0:T(8,128)S(1)}, f32[1,128]{1,0:T(1,128)S(1)}, f32[128,384]{1,0:T(8,128)S(1)}, f32[1,128]{1,0:T(1,128)S(1)}, f32[4,384]{1,0:T(4,128)S(1)}, /*index=5*/f32[4,1]{1,0:T(4,128)S(1)}) custom-call(f32[128,384]{1,0:T(8,128)S(1)} %bitcast.14, f32[1,128]{1,0:T(1,128)S(1)} %bitcast.18, f32[128,384]{1,0:T(8,128)S(1)} %bitcast.15, ...), custom_call_target="tpu_custom_call" | custom-call | tf_op jit(solution)/shard_map/pallas_call | solution.py:379
  83.6 0.6 reduce
  84.2 0.7 copy.24
  84.9 0.5 copy.25
  85.4 0.7 copy.26
  86.1 0.5 copy.27
  86.6 0.6 copy.28
  (1 shorter events, 0.0 us)
Async XLA Ops:
  2.9 1.9 %copy-start = (f32[2048,384]{1,0:T(8,128)S(1)}, f32[2048,384]{1,0:T(8,128)}, u32[]{:S(2)}) copy-start(f32[2048,384]{1,0:T(8,128)} %rel_hbm.1) | copy-start | bytes 9437188
  4.8 0.9 %copy-start.1 = (f32[1,1,128,384]{3,2,1,0:T(8,128)S(1)}, f32[1,1,128,384]{3,2,1,0:T(8,128)}, u32[]{:S(2)}) copy-start(f32[1,1,128,384]{3,2,1,0:T(8,128)} %param.11) | copy-start | bytes 589828
  5.7 0.9 %copy-start.2 = (f32[1,1,128,384]{3,2,1,0:T(8,128)S(1)}, f32[1,1,128,384]{3,2,1,0:T(8,128)}, u32[]{:S(2)}) copy-start(f32[1,1,128,384]{3,2,1,0:T(8,128)} %param.13) | copy-start | bytes 589828
  6.6 0.7 copy-start.3
  7.3 0.7 copy-start.4

commit v3 on v2

--- a/solution.py
+++ b/solution.py
@@ -12,6 +12,7 @@
 SIZE = {"x": 4, "y": 8, "z": 8}
 ROUND = ((2, 0), (0, 0), (1, 0), (2, 1), (0, 1), (1, 1), (2, 2), (0, 2), (1, 2))
 STEPS = 3
+VMEM_LIMIT = 60 * 2**20
 EDGES_1, EDGES_2, NEXT, SRC_END, DST_END = (0, 31), (0, 30), (1, 31), (1, 2), (0, 3)
 
 
@@ -63,16 +64,16 @@
     return 1.0 / (1.0 + jnp.exp(-value))
 
 
-def eye():
-    return lax.broadcasted_iota(I32, (128, 128), 0) == lax.broadcasted_iota(I32, (128, 128), 1)
+def eye(n):
+    return lax.broadcasted_iota(I32, (n, n), 0) == lax.broadcasted_iota(I32, (n, n), 1)
 
 
 def as_column(row):
-    return jnp.sum(jnp.where(eye(), row, 0.0), axis=1, keepdims=True)
+    return jnp.sum(jnp.where(eye(row.shape[1]), row, 0.0), axis=1, keepdims=True)
 
 
 def as_row(column):
-    return jnp.sum(jnp.where(eye(), column, 0.0), axis=0, keepdims=True)
+    return jnp.sum(jnp.where(eye(column.shape[0]), column, 0.0), axis=0, keepdims=True)
 
 
 def adagrad(block, state_row, grad):
@@ -91,23 +92,39 @@
 
 
 def window_kernel(
-    src_ref, src_st_ref, dst_ref, dst_st_ref, rel_hbm, rel_st_ref, idx_ref,
+    src_hbm, src_st_hbm, dst_hbm, dst_st_hbm, rel_hbm, rel_st_hbm, s_hbm, d_hbm, r_hbm, n_hbm, count_hbm,
     src_out, src_st_out, dst_out, dst_st_out, rel_out, rel_st_out,
-    table, idx, idx_sib, idx_smem, src_in, src_st_in, src_new, src_st_new, dst_cur, dst_st_cur,
+    table, rel_st, s_raw, d_raw, r_raw, n_raw, r_smem, count_smem,
+    idx_mine, idx, idx_sib, idx_smem, src_in, src_st_in, src_new, src_st_new, dst_cur, dst_st_cur,
     rel_vec, v_own, v_sib, half, *rest,
 ):
     recv = {(c, p): rest[c * 3 + p] for c in range(3) for p in range(3)}
     held = {(c, p): rest[9 + c * 2 + p] for c in range(3) for p in range(2)}
-    (table_sem, smem_sem, idx_sem, sib_idx_sem, block_sem, state_sem, v_sem, end_sem,
+    (load_sem, smem_sem, idx_sem, sib_idx_sem, block_sem, state_sem, v_sem, end_sem,
      send_sem, recv_sem) = rest[15:]
     me = coords()
     sibling = device_of({**me, "core": 1 - me["core"]})
 
-    load_table = pltpu.make_async_copy(rel_hbm, table, table_sem)
-    load_table.start()
+    loads = [
+        pltpu.make_async_copy(source, target, load_sem.at[i])
+        for i, (source, target) in enumerate(
+            [
+                (r_hbm, r_smem), (count_hbm, count_smem), (rel_hbm, table),
+                (s_hbm, s_raw), (d_hbm, d_raw), (r_hbm, r_raw), (n_hbm, n_raw),
+                (src_hbm, src_in.at[0]), (dst_hbm, dst_cur),
+                (src_st_hbm, src_st_in.at[0]), (dst_st_hbm, dst_st_cur), (rel_st_hbm, rel_st),
+            ]
+        )
+    ]
+    for load in loads:
+        load.start()
 
     barrier = pltpu.get_barrier_semaphore()
     pl.semaphore_signal(barrier, inc=1, device_id=sibling, device_id_type=MESH)
+    for ds, dd in (NEXT, EDGES_1, EDGES_2, SRC_END, DST_END):
+        for offset in ((ds, dd), ((16 - ds) % 16, (32 - dd) % 32)):
+            pl.semaphore_signal(barrier, inc=1, device_id=moved(offset), device_id_type=MESH)
+
     for axis in "xyz":
 
         @pl.loop(1, SIZE[axis])
@@ -116,17 +133,19 @@
                 barrier, inc=1, device_id=partner(me, axis, o), device_id_type=MESH
             )
 
-    for ds, dd in (EDGES_1, EDGES_2, NEXT, SRC_END, DST_END):
-        for offset in ((ds, dd), ((16 - ds) % 16, (32 - dd) % 32)):
-            pl.semaphore_signal(barrier, inc=1, device_id=moved(offset), device_id_type=MESH)
-
-    idx[0] = idx_ref[0]
-    src_in[0] = src_ref[...]
-    src_st_in[0] = src_st_ref[...]
-    dst_cur[...] = dst_ref[...]
-    dst_st_cur[...] = dst_st_ref[...]
     half[...] = jnp.zeros_like(half)
-    pl.semaphore_wait(barrier, 28)
+    for load in loads:
+        load.wait()
+    block_of = lax.broadcasted_iota(I32, (1, 256), 1) >> 7
+    for t in range(STEPS):
+        idx_mine[t, 0:1, :] = s_raw[t]
+        idx_mine[t, 1:2, :] = d_raw[t]
+        idx_mine[t, 2:3, :] = r_raw[t]
+        idx_mine[t, 3:4, 0:128] = n_raw[t, 0:1, :]
+        idx_mine[t, 3:4, 128:256] = n_raw[t, 1:2, :]
+        live = jnp.where(block_of < count_smem[0, t], 1, 0)
+        idx_mine[t, 4:8, :] = jnp.broadcast_to(live, (4, 256))
+    idx[0] = idx_mine[0]
 
     def remote(source, target, sems, to):
         return pltpu.make_async_remote_copy(
@@ -134,7 +153,7 @@
         )
 
     def edge_copy(t, offset):
-        return remote(idx_ref.at[t], idx.at[t], idx_sem.at[t], moved(offset))
+        return remote(idx_mine.at[t], idx.at[t], idx_sem.at[t], moved(offset))
 
     def sib_idx_copy(t):
         return remote(idx.at[t], idx_sib.at[t], sib_idx_sem.at[t], sibling)
@@ -148,21 +167,19 @@
     def state_copy(t):
         return remote(src_st_new.at[t], src_st_in.at[t + 1], state_sem.at[t], moved(NEXT))
 
-    edges = (None, edge_copy(1, EDGES_1), edge_copy(2, EDGES_2))
-    edges[1].start()
-    edges[2].start()
-    sib_idx_copy(0).start()
-
-    def gather_relations(t):
-        load = pltpu.make_async_copy(idx.at[t], idx_smem.at[t], smem_sem)
-        load.start()
-        load.wait()
-
+    ends = [
+        remote(src_st_new.at[2], src_st_out, end_sem.at[0], moved(SRC_END)),
+        remote(src_new.at[2], src_out, end_sem.at[1], moved(SRC_END)),
+        remote(dst_st_cur, dst_st_out, end_sem.at[2], moved(DST_END)),
+        remote(dst_cur, dst_out, end_sem.at[3], moved(DST_END)),
+    ]
+
+    def gather_relations(row_of):
         @pl.loop(0, 32)
         def _(i):
             for j in range(8):
                 e = i * 8 + j
-                rel_vec[pl.ds(e, 1), :] = table[pl.ds(idx_smem[t, 2, e], 1), :]
+                rel_vec[pl.ds(e, 1), :] = table[pl.ds(row_of(e), 1), :]
 
     def add_third(t, c):
         v = jnp.concatenate(
@@ -179,7 +196,7 @@
             both = dot(hot, rhs)
             half[c, rows, :] += both[:, :128] + both[:, 128:]
 
-    def work(t):
+    def work(t, send_v, send_src):
         rows = idx[t]
         columns = jnp.transpose(rows.astype(F32)).astype(I32)
         s_col, d_col, n_col = columns[:, 0:1], columns[:, 1:2], columns[:, 3:4]
@@ -204,7 +221,7 @@
             rows_part.append(dot(jnp.transpose(gneg).astype(BF16), ab[block]))
         gprod = gpos * dst_vec + jnp.concatenate(negs_part, axis=0)
         v_own[t] = gprod * src_vec
-        v_copy(t).start()
+        send_v()
         subl = lax.broadcasted_iota(I32, (128, 256), 0)
         s_hot = one_hot(subl == rows[0:1])
         grad_src = dot(jnp.concatenate([s_hot, s_hot], axis=1), split(gprod * rel))
@@ -212,11 +229,7 @@
         src_new[t] = block
         src_st_new[t] = state
 
-        @pl.when(t < 2)
-        def _():
-            state_copy(t).start()
-            block_copy(t).start()
-
+        send_src()
         d_hot = one_hot(subl == rows[1:2])
         n_hot = one_hot(subl == rows[3:4])
         grad_dst = dot(
@@ -227,34 +240,51 @@
         dst_cur[...] = block
         dst_st_cur[...] = state
 
-    load_table.wait()
-
-    @pl.loop(0, STEPS)
+    def enter():
+        pl.semaphore_wait(barrier, 28)
+
+    def first_sends():
+        enter()
+        state_copy(0).start()
+        block_copy(0).start()
+        edge_copy(1, EDGES_1).start()
+        edge_copy(2, EDGES_2).start()
+        sib_idx_copy(0).start()
+        v_copy(0).start()
+
+    gather_relations(lambda e: r_smem[0, 0, e])
+    work(0, lambda: None, first_sends)
+
+    @pl.loop(1, STEPS)
     def _(t):
-        @pl.when(t > 0)
-        def _():
-            edge_copy(t, EDGES_1).wait()
-            sib_idx_copy(t).start()
-
-        gather_relations(t)
-
-        @pl.when(t > 0)
-        def _():
-            sib_idx_copy(t - 1).wait()
-            v_copy(t - 1).wait()
-            for c in range(3):
-                add_third(t - 1, c)
-            state_copy(t - 1).wait()
-            block_copy(t - 1).wait()
-
-        work(t)
-
-    ends = [
-        remote(src_st_new.at[2], src_st_out, end_sem.at[0], moved(SRC_END)),
-        remote(dst_st_cur, dst_st_out, end_sem.at[1], moved(DST_END)),
-        remote(src_new.at[2], src_out, end_sem.at[2], moved(SRC_END)),
-        remote(dst_cur, dst_out, end_sem.at[3], moved(DST_END)),
-    ]
+        edge_copy(t, EDGES_1).wait()
+        sib_idx_copy(t).start()
+        load = pltpu.make_async_copy(idx.at[t], idx_smem.at[t], smem_sem)
+        load.start()
+        load.wait()
+        gather_relations(lambda e: idx_smem[t, 2, e])
+        sib_idx_copy(t - 1).wait()
+        v_copy(t - 1).wait()
+        for c in range(3):
+            add_third(t - 1, c)
+        state_copy(t - 1).wait()
+        block_copy(t - 1).wait()
+
+        def send_src():
+            @pl.when(t < 2)
+            def _():
+                state_copy(t).start()
+                block_copy(t).start()
+
+            @pl.when(t == 2)
+            def _():
+                ends[0].start()
+                ends[1].start()
+
+        work(t, v_copy(t).start, send_src)
+
+    ends[2].start()
+    ends[3].start()
 
     def rows_of(c, p, j):
         if p == 2:
@@ -298,8 +328,6 @@
     for c in (2, 0, 1):
         add_third(2, c)
         start_phase(c, 0)
-    for copy in ends:
-        copy.start()
     last = {}
     for c, p in ROUND:
         total = finish_phase(c, p)
@@ -313,11 +341,24 @@
     owner = lax.axis_index("src") * 32 + lax.axis_index("dst")
     near = table[pl.ds(pl.multiple_of(lax.div(owner, 2) * 8, 8), 8), :]
     own = jnp.where(lax.rem(owner, 2) == 0, near[0:4], near[4:8])
-    state = rel_st_ref[...] + jnp.sum(grad * grad, axis=1, keepdims=True) * (1.0 / 384)
-    rel_st_out[...] = state
+    state = as_column(rel_st[...]) + jnp.sum(grad * grad, axis=1, keepdims=True) * (1.0 / 384)
+    rel_st_out[...] = as_row(state)
     rel_out[...] = own - 0.1 * grad / jnp.sqrt(state)
     for copy in ends:
         copy.wait()
+
+
+def store_kernel(*refs):
+    sources, targets, held, sems = refs[:6], refs[6:12], refs[12:18], refs[18]
+    loads = [pltpu.make_async_copy(sources[i], held[i], sems.at[0, i]) for i in range(6)]
+    stores = [pltpu.make_async_copy(held[i], targets[i], sems.at[1, i]) for i in range(6)]
+    for load in loads:
+        load.start()
+    for load, store in zip(loads, stores):
+        load.wait()
+        store.start()
+    for store in stores:
+        store.wait()
 
 
 def on_device(
@@ -333,25 +374,18 @@
     negative_block_rows,
     bucket_block_counts,
 ):
-    counts = bucket_block_counts[0, 0]
-    live = (jnp.arange(256, dtype=I32)[None, :] // 128 < counts[:, None]).astype(I32)
-    idx = jnp.stack(
-        [
-            source_edge_rows[0, 0],
-            destination_edge_rows[0, 0],
-            edge_relation_index[0, 0],
-            negative_block_rows[0, 0].reshape(STEPS, 256),
-            live,
-            live,
-            live,
-            live,
-        ],
-        axis=1,
-    )
-    vmem = pl.BlockSpec(memory_space=pltpu.VMEM)
+    vmem, hbm = pl.BlockSpec(memory_space=pltpu.VMEM), pl.BlockSpec(memory_space=pl.ANY)
     dma = pltpu.SemaphoreType.DMA
     scratch = [
         pltpu.VMEM((2048, 384), F32),
+        pltpu.VMEM((1, 4), F32),
+        pltpu.VMEM((3, 1, 256), I32),
+        pltpu.VMEM((3, 1, 256), I32),
+        pltpu.VMEM((3, 1, 256), I32),
+        pltpu.VMEM((3, 2, 128), I32),
+        pltpu.SMEM((3, 1, 256), I32),
+        pltpu.SMEM((1, 3), I32),
+        pltpu.VMEM((3, 8, 256), I32),
         pltpu.VMEM((3, 8, 256), I32),
         pltpu.VMEM((3, 8, 256), I32),
         pltpu.SMEM((3, 8, 256), I32),
@@ -372,25 +406,20 @@
     for c in range(3):
         for p in range(2):
             scratch.append(pltpu.VMEM((CHUNK[c][p], 128), F32))
-    scratch += [dma, dma, dma((3, 2)), dma((3, 2)), dma((2, 2)), dma((2, 2)), dma((3, 2)), dma((4, 2))]
+    scratch += [dma((12,)), dma, dma((3, 2)), dma((3, 2)), dma((2, 2)), dma((2, 2)), dma((3, 2)), dma((4, 2))]
     scratch += [dma((3, 3)), dma((3, 3))]
     block = jax.ShapeDtypeStruct((128, 384), F32)
     row = jax.ShapeDtypeStruct((1, 128), F32)
-    src_out, src_st, dst_out, dst_st, rel_out, rel_st = pl.pallas_call(
+    results = (block, row, block, row)
+    results += (jax.ShapeDtypeStruct((4, 384), F32), jax.ShapeDtypeStruct((1, 4), F32))
+    outs = pl.pallas_call(
         window_kernel,
-        out_shape=(
-            block,
-            row,
-            block,
-            row,
-            jax.ShapeDtypeStruct((4, 384), F32),
-            jax.ShapeDtypeStruct((4, 1), F32),
-        ),
-        in_specs=[vmem, vmem, vmem, vmem, pl.BlockSpec(memory_space=pl.ANY), vmem, vmem],
+        out_shape=results,
+        in_specs=[hbm] * 11,
         out_specs=(vmem,) * 6,
         scratch_shapes=scratch,
         compiler_params=pltpu.CompilerParams(
-            collective_id=0, has_side_effects=True, vmem_limit_bytes=40 * 2**20
+            collective_id=0, has_side_effects=True, vmem_limit_bytes=VMEM_LIMIT
         ),
     )(
         source_embedding_table[0, 0],
@@ -398,16 +427,28 @@
         destination_embedding_table[0, 0],
         destination_adagrad_state[0],
         relations,
-        rel_state[:, None],
-        idx,
-    )
+        rel_state[None],
+        source_edge_rows.reshape(STEPS, 1, 256),
+        destination_edge_rows.reshape(STEPS, 1, 256),
+        edge_relation_index.reshape(STEPS, 1, 256),
+        negative_block_rows[0, 0],
+        bucket_block_counts[0],
+    )
+    src_out, src_st, dst_out, dst_st, rel_out, rel_st = pl.pallas_call(
+        store_kernel,
+        out_shape=results,
+        in_specs=[hbm] * 6,
+        out_specs=(hbm,) * 6,
+        scratch_shapes=[pltpu.VMEM(r.shape, F32) for r in results] + [dma((2, 6))],
+        compiler_params=pltpu.CompilerParams(vmem_limit_bytes=VMEM_LIMIT),
+    )(*outs)
     return (
         src_out[None, None],
         src_st[None],
         dst_out[None, None],
         dst_st[None],
         rel_out,
-        rel_st[:, 0],
+        rel_st[0],
     )
 
 

time: 87.5 us -> 74.1 us (0.85)
  the two profiles are of different devices: /device:TPU:1 before, /device:TPU:6 now
where the time goes in v3:
time: 74.1 us; the launch traced here: 74 us
  Pallas kernels  73.3 us (99%)
    pallas_call x1, Pallas kernels, on_device(): pl.pallas_call(window_kernel, out_shape=results, in_specs=[hbm] * 11, out...  71.5 us
    pallas_call x1, Pallas kernels, on_device(): pl.pallas_call(store_kernel, out_shape=results, in_specs=[hbm] * 6, out_s...  1.81 us

profile of v3, /device:TPU:6, one launch (start us, length us, event | category | flops | bytes accessed | tf_op | source)
XLA Modules:
  0.0 74.0 jit_solution(14061262815111527004)
XLA Ops:
  0.6 71.5 %shard_map.154 = (f32[128,384]{1,0:T(8,128)}, f32[1,128]{1,0:T(1,128)}, f32[128,384]{1,0:T(8,128)}, f32[1,128]{1,0:T(1,128)}, f32[4,384]{1,0:T(4,128)}, /*index=5*/f32[1,4]{1,0:T(1,128)}) custom-call(f32[128,384]{1,0:T(8,128)} %bitcast.15, f32[1,128]{1,0:T(1,128)} %bitcast.21, f32[128,384]{1,0:T(8,128)} %bitcast.16, f32[1,128]{1,0:T(1,128)} %bitcast.22, ...), custom_call_target="tpu_custom_call" | custom-call | tf_op jit(solution)/shard_map/pallas_call | solution.py:415
  72.1 1.8 %shard_map.155 = (f32[128,384]{1,0:T(8,128)}, f32[1,128]{1,0:T(1,128)}, f32[128,384]{1,0:T(8,128)}, f32[1,128]{1,0:T(1,128)}, f32[4,384]{1,0:T(4,128)}, /*index=5*/f32[1,4]{1,0:T(1,128)}) custom-call(f32[128,384]{1,0:T(8,128)} %get-tuple-element.18.refs_0_, f32[1,128]{1,0:T(1,128)} %get-tuple-element.19.refs_1_, f32[128,384]{1,0:T(8,128)} %get-tuple-element.20.refs_2_, ...), custom_call_target="tpu_custom_call" | custom-call | tf_op jit(solution)/shard_map/pallas_call | solution.py:437

commit v4 on v3

--- a/solution.py
+++ b/solution.py
@@ -7,10 +7,9 @@
 
 MESH = pl.DeviceIdType.MESH
 F32, BF16, I32 = jnp.float32, jnp.bfloat16, jnp.int32
-ORDERS = (("z", "y", "x"), ("y", "x", "z"), ("x", "z", "y"))
-CHUNK = ((128, 16, 8), (128, 32, 8), (256, 32, 8))
+ORDERS = (("z", "y"), ("y", "z"), ("z", "y"))
 SIZE = {"x": 4, "y": 8, "z": 8}
-ROUND = ((2, 0), (0, 0), (1, 0), (2, 1), (0, 1), (1, 1), (2, 2), (0, 2), (1, 2))
+THIRDS = (0, 2, 1)
 STEPS = 3
 VMEM_LIMIT = 60 * 2**20
 EDGES_1, EDGES_2, NEXT, SRC_END, DST_END = (0, 31), (0, 30), (1, 31), (1, 2), (0, 3)
@@ -84,11 +83,8 @@
 def positions(r, c):
     k, z, x = r & 3, (r >> 4) & 7, (r >> 8) & 3
     y = ((r >> 10) << 2) | ((r >> 2) & 3)
-    if c == 0:
-        return (((z * 8 + y) * 4 + x) * 4) + k
-    if c == 1:
-        return (((y * 4 + x) * 8 + z) * 4) + k
-    return (((x * 8 + z) * 8 + y) * 4) + k
+    near, far = (z, y) if ORDERS[c][0] == "z" else (y, z)
+    return (((x * 8 + near) * 8 + far) * 4) + k
 
 
 def window_kernel(
@@ -98,10 +94,9 @@
     idx_mine, idx, idx_sib, idx_smem, src_in, src_st_in, src_new, src_st_new, dst_cur, dst_st_cur,
     rel_vec, v_own, v_sib, half, *rest,
 ):
-    recv = {(c, p): rest[c * 3 + p] for c in range(3) for p in range(3)}
-    held = {(c, p): rest[9 + c * 2 + p] for c in range(3) for p in range(2)}
+    relay_in, near_in, recv, held = rest[0], rest[1], rest[2:4], rest[4:6]
     (load_sem, smem_sem, idx_sem, sib_idx_sem, block_sem, state_sem, v_sem, end_sem,
-     send_sem, recv_sem) = rest[15:]
+     x_sem, ring_sem) = rest[6:]
     me = coords()
     sibling = device_of({**me, "core": 1 - me["core"]})
 
@@ -286,64 +281,90 @@
     ends[2].start()
     ends[3].start()
 
-    def rows_of(c, p, j):
-        if p == 2:
+    ahead, across, behind = (lax.rem(me["x"] + o, 4) for o in (1, 2, 3))
+
+    def x_copy(c, k):
+        lower, upper = 0, 128
+        chunk, first, target, step = (
+            (across, lower, relay_in.at[c, 0], 1),
+            (across, upper, relay_in.at[c, 1], 3),
+            (ahead, upper, near_in.at[c, 0], 1),
+            (behind, lower, near_in.at[c, 1], 3),
+            (ahead, lower, near_in.at[c, 2], 1),
+            (behind, upper, near_in.at[c, 3], 3),
+        )[k]
+        source = half.at[c, pl.ds(pl.multiple_of(chunk * 256 + first, 128), 128)]
+        return remote(source, target, x_sem.at[c, k], partner(me, "x", step))
+
+    def ring_rows(p, j):
+        if p == 1:
             return pl.ds(pl.multiple_of(lax.div(j, 2) * 8, 8), 8)
-        return pl.ds(pl.multiple_of(j * CHUNK[c][p], CHUNK[c][p]), CHUNK[c][p])
-
-    def start_phase(c, p):
+        return pl.ds(pl.multiple_of(j * 32, 32), 32)
+
+    def ring_start(c, p):
         axis = ORDERS[c][p]
-        source = half.at[c] if p == 0 else held[c, p - 1]
-
-        @pl.loop(1, SIZE[axis])
-        def _(o):
-            target = lax.rem(me[axis] + o, SIZE[axis])
+        for o in range(1, 8):
+            target = lax.rem(me[axis] + o, 8)
             pltpu.make_async_remote_copy(
-                source.at[rows_of(c, p, target)],
-                recv[c, p].at[o - 1],
-                send_sem.at[c, p],
-                recv_sem.at[c, p],
+                held[p].at[c, ring_rows(p, target)],
+                recv[p].at[c, o - 1],
+                ring_sem.at[c, p, 0],
+                ring_sem.at[c, p, 1],
                 device_id=partner(me, axis, o),
                 device_id_type=MESH,
             ).start()
 
-    def finish_phase(c, p):
-        axis = ORDERS[c][p]
-        pltpu.make_async_remote_copy(
-            recv[c, p],
-            recv[c, p],
-            send_sem.at[c, p],
-            recv_sem.at[c, p],
-            device_id=sibling,
-            device_id_type=MESH,
-        ).wait()
-        source = half.at[c] if p == 0 else held[c, p - 1]
-        total = source[rows_of(c, p, me[axis]), :]
-        for o in range(SIZE[axis] - 1):
-            total = total + recv[c, p][o]
+    def ring_all(c, p):
+        return remote(recv[p].at[c], recv[p].at[c], ring_sem.at[c, p], sibling)
+
+    def ring_finish(c, p):
+        ring_all(c, p).wait_recv()
+        total = held[p][c, ring_rows(p, me[ORDERS[c][p]]), :]
+        for o in range(7):
+            total = total + recv[p][c, o]
         return total
 
     sib_idx_copy(2).wait()
     v_copy(2).wait()
-    for c in (2, 0, 1):
+    for c in THIRDS:
         add_third(2, c)
-        start_phase(c, 0)
+        for k in range(4):
+            x_copy(c, k).start()
+    for c in THIRDS:
+        for k, chunk, first in ((0, ahead, 0), (1, behind, 128)):
+            x_copy(c, k).wait_recv()
+            rows = pl.ds(pl.multiple_of(chunk * 256 + first, 128), 128)
+            half[c, rows, :] += relay_in[c, k]
+            x_copy(c, 4 + k).start()
+    own = pl.multiple_of(me["x"] * 256, 256)
+    for c in THIRDS:
+        for k in range(2, 6):
+            x_copy(c, k).wait_recv()
+        held[0][c, 0:128, :] = half[c, pl.ds(own, 128), :] + near_in[c, 1] + near_in[c, 2]
+        held[0][c, 128:256, :] = (
+            half[c, pl.ds(pl.multiple_of(own + 128, 128), 128), :] + near_in[c, 0] + near_in[c, 3]
+        )
+        ring_start(c, 0)
+    for c in THIRDS:
+        held[1][c] = ring_finish(c, 0)
+        ring_start(c, 1)
     last = {}
-    for c, p in ROUND:
-        total = finish_phase(c, p)
-        if p < 2:
-            held[c, p][...] = total
-            start_phase(c, p + 1)
-        else:
-            odd = lax.rem(me[ORDERS[c][2]], 2)
-            last[c] = jnp.where(odd == 0, total[0:4], total[4:8])
+    for c in THIRDS:
+        total = ring_finish(c, 1)
+        odd = lax.rem(me[ORDERS[c][1]], 2)
+        last[c] = jnp.where(odd == 0, total[0:4], total[4:8])
     grad = jnp.concatenate([last[0], last[1], last[2]], axis=1)
     owner = lax.axis_index("src") * 32 + lax.axis_index("dst")
     near = table[pl.ds(pl.multiple_of(lax.div(owner, 2) * 8, 8), 8), :]
-    own = jnp.where(lax.rem(owner, 2) == 0, near[0:4], near[4:8])
+    own_rel = jnp.where(lax.rem(owner, 2) == 0, near[0:4], near[4:8])
     state = as_column(rel_st[...]) + jnp.sum(grad * grad, axis=1, keepdims=True) * (1.0 / 384)
     rel_st_out[...] = as_row(state)
-    rel_out[...] = own - 0.1 * grad / jnp.sqrt(state)
+    rel_out[...] = own_rel - 0.1 * grad / jnp.sqrt(state)
+    for c in THIRDS:
+        for k in range(6):
+            x_copy(c, k).wait_send()
+        for p in range(2):
+            ring_all(c, p).wait_send()
     for copy in ends:
         copy.wait()
 
@@ -400,14 +421,16 @@
         pltpu.VMEM((3, 256, 384), F32),
         pltpu.VMEM((3, 1024, 128), F32),
     ]
-    for c in range(3):
-        for p in range(3):
-            scratch.append(pltpu.VMEM((SIZE[ORDERS[c][p]] - 1, CHUNK[c][p], 128), F32))
-    for c in range(3):
-        for p in range(2):
-            scratch.append(pltpu.VMEM((CHUNK[c][p], 128), F32))
+    scratch += [
+        pltpu.VMEM((3, 2, 128, 128), F32),
+        pltpu.VMEM((3, 4, 128, 128), F32),
+        pltpu.VMEM((3, 7, 32, 128), F32),
+        pltpu.VMEM((3, 7, 8, 128), F32),
+        pltpu.VMEM((3, 256, 128), F32),
+        pltpu.VMEM((3, 32, 128), F32),
+    ]
     scratch += [dma((12,)), dma, dma((3, 2)), dma((3, 2)), dma((2, 2)), dma((2, 2)), dma((3, 2)), dma((4, 2))]
-    scratch += [dma((3, 3)), dma((3, 3))]
+    scratch += [dma((3, 6, 2)), dma((3, 2, 2))]
     block = jax.ShapeDtypeStruct((128, 384), F32)
     row = jax.ShapeDtypeStruct((1, 128), F32)
     results = (block, row, block, row)

time: 74.1 us -> 69.9 us (0.943)
  the two profiles are of different devices: /device:TPU:6 before, /device:TPU:48 now
where the time goes in v4:
time: 69.9 us; the launch traced here: 69.8 us
  Pallas kernels  69.2 us (99%)
    pallas_call x1, Pallas kernels, on_device(): pl.pallas_call(window_kernel, out_shape=results, in_specs=[hbm] * 11, out...  67.3 us
    pallas_call x1, Pallas kernels, on_device(): pl.pallas_call(store_kernel, out_shape=results, in_specs=[hbm] * 6, out_s...  1.81 us

profile of v4, /device:TPU:48, one launch (start us, length us, event | category | flops | bytes accessed | tf_op | source)
XLA Modules:
  0.0 69.8 jit_solution(11739251222634937616)
XLA Ops:
  0.6 67.3 %shard_map.154 = (f32[128,384]{1,0:T(8,128)}, f32[1,128]{1,0:T(1,128)}, f32[128,384]{1,0:T(8,128)}, f32[1,128]{1,0:T(1,128)}, f32[4,384]{1,0:T(4,128)}, /*index=5*/f32[1,4]{1,0:T(1,128)}) custom-call(f32[128,384]{1,0:T(8,128)} %bitcast.15, f32[1,128]{1,0:T(1,128)} %bitcast.21, f32[128,384]{1,0:T(8,128)} %bitcast.16, f32[1,128]{1,0:T(1,128)} %bitcast.22, ...), custom_call_target="tpu_custom_call" | custom-call | tf_op jit(solution)/shard_map/pallas_call | solution.py:438
  68.0 1.8 %shard_map.155 = (f32[128,384]{1,0:T(8,128)}, f32[1,128]{1,0:T(1,128)}, f32[128,384]{1,0:T(8,128)}, f32[1,128]{1,0:T(1,128)}, f32[4,384]{1,0:T(4,128)}, /*index=5*/f32[1,4]{1,0:T(1,128)}) custom-call(f32[128,384]{1,0:T(8,128)} %get-tuple-element.18.refs_0_, f32[1,128]{1,0:T(1,128)} %get-tuple-element.19.refs_1_, f32[128,384]{1,0:T(8,128)} %get-tuple-element.20.refs_2_, ...), custom_call_target="tpu_custom_call" | custom-call | tf_op jit(solution)/shard_map/pallas_call | solution.py:460

commit v5 on v4

--- a/solution.py
+++ b/solution.py
@@ -7,9 +7,10 @@
 
 MESH = pl.DeviceIdType.MESH
 F32, BF16, I32 = jnp.float32, jnp.bfloat16, jnp.int32
-ORDERS = (("z", "y"), ("y", "z"), ("z", "y"))
+ORDERS = (("z", "y", "x"), ("x", "y", "z"), ("x", "z", "y"))
 SIZE = {"x": 4, "y": 8, "z": 8}
 THIRDS = (0, 2, 1)
+ALONG_X = (2, 1)
 STEPS = 3
 VMEM_LIMIT = 60 * 2**20
 EDGES_1, EDGES_2, NEXT, SRC_END, DST_END = (0, 31), (0, 30), (1, 31), (1, 2), (0, 3)
@@ -83,8 +84,9 @@
 def positions(r, c):
     k, z, x = r & 3, (r >> 4) & 7, (r >> 8) & 3
     y = ((r >> 10) << 2) | ((r >> 2) & 3)
-    near, far = (z, y) if ORDERS[c][0] == "z" else (y, z)
-    return (((x * 8 + near) * 8 + far) * 4) + k
+    at = {"x": x, "y": y, "z": z}
+    first, second, third = ORDERS[c]
+    return ((at[first] * SIZE[second] + at[second]) * SIZE[third] + at[third]) * 4 + k
 
 
 def window_kernel(
@@ -95,8 +97,9 @@
     rel_vec, v_own, v_sib, half, *rest,
 ):
     relay_in, near_in, recv, held = rest[0], rest[1], rest[2:4], rest[4:6]
+    z_relay, z_part, z_near = rest[6:9]
     (load_sem, smem_sem, idx_sem, sib_idx_sem, block_sem, state_sem, v_sem, end_sem,
-     x_sem, ring_sem) = rest[6:]
+     x_sem, z_sem, ring_sem) = rest[9:]
     me = coords()
     sibling = device_of({**me, "core": 1 - me["core"]})
 
@@ -153,8 +156,12 @@
     def sib_idx_copy(t):
         return remote(idx.at[t], idx_sib.at[t], sib_idx_sem.at[t], sibling)
 
-    def v_copy(t):
-        return remote(v_own.at[t], v_sib.at[t], v_sem.at[t], sibling)
+    def v_copy(t, c):
+        return remote(v_own.at[t, c], v_sib.at[t, c], v_sem.at[t, c], sibling)
+
+    def send_v(t):
+        for c in THIRDS:
+            v_copy(t, c).start()
 
     def block_copy(t):
         return remote(src_new.at[t], src_in.at[t + 1], block_sem.at[t], moved(NEXT))
@@ -178,7 +185,7 @@
 
     def add_third(t, c):
         v = jnp.concatenate(
-            [v_own[t, :, c * 128 : (c + 1) * 128], v_sib[t, :, c * 128 : (c + 1) * 128]], axis=0
+            [v_own[t, c], v_sib[t, c]], axis=0
         )
         rhs = split(v, axis=1)
         r = jnp.concatenate([idx[t, 2:3, :], idx_sib[t, 2:3, :]], axis=1)
@@ -191,7 +198,7 @@
             both = dot(hot, rhs)
             half[c, rows, :] += both[:, :128] + both[:, 128:]
 
-    def work(t, send_v, send_src):
+    def work(t, send_values, send_src):
         rows = idx[t]
         columns = jnp.transpose(rows.astype(F32)).astype(I32)
         s_col, d_col, n_col = columns[:, 0:1], columns[:, 1:2], columns[:, 3:4]
@@ -215,8 +222,10 @@
             negs_part.append(dot(gneg.astype(BF16), negb[block]))
             rows_part.append(dot(jnp.transpose(gneg).astype(BF16), ab[block]))
         gprod = gpos * dst_vec + jnp.concatenate(negs_part, axis=0)
-        v_own[t] = gprod * src_vec
-        send_v()
+        v = gprod * src_vec
+        for c in range(3):
+            v_own[t, c] = v[:, c * 128 : (c + 1) * 128]
+        send_values()
         subl = lax.broadcasted_iota(I32, (128, 256), 0)
         s_hot = one_hot(subl == rows[0:1])
         grad_src = dot(jnp.concatenate([s_hot, s_hot], axis=1), split(gprod * rel))
@@ -245,7 +254,7 @@
         edge_copy(1, EDGES_1).start()
         edge_copy(2, EDGES_2).start()
         sib_idx_copy(0).start()
-        v_copy(0).start()
+        send_v(0)
 
     gather_relations(lambda e: r_smem[0, 0, e])
     work(0, lambda: None, first_sends)
@@ -258,10 +267,6 @@
         load.start()
         load.wait()
         gather_relations(lambda e: idx_smem[t, 2, e])
-        sib_idx_copy(t - 1).wait()
-        v_copy(t - 1).wait()
-        for c in range(3):
-            add_third(t - 1, c)
         state_copy(t - 1).wait()
         block_copy(t - 1).wait()
 
@@ -276,10 +281,17 @@
                 ends[0].start()
                 ends[1].start()
 
-        work(t, v_copy(t).start, send_src)
-
-    ends[2].start()
-    ends[3].start()
+        work(t, lambda: send_v(t), send_src)
+
+        @pl.when(t == 2)
+        def _():
+            ends[2].start()
+            ends[3].start()
+
+        sib_idx_copy(t - 1).wait()
+        for c in THIRDS:
+            v_copy(t - 1, c).wait()
+            add_third(t - 1, c)
 
     ahead, across, behind = (lax.rem(me["x"] + o, 4) for o in (1, 2, 3))
 
@@ -296,18 +308,42 @@
         source = half.at[c, pl.ds(pl.multiple_of(chunk * 256 + first, 128), 128)]
         return remote(source, target, x_sem.at[c, k], partner(me, "x", step))
 
-    def ring_rows(p, j):
+    z_at = [lax.rem(me["z"] + o, 8) for o in range(8)]
+
+    def z_rows(chunk, first, count):
+        return pl.ds(pl.multiple_of(z_at[chunk] * 128 + first, count), count)
+
+    def z_copy(k):
+        chunk, first, count, target, step = (
+            (3, 0, 128, z_relay.at[0], 1),
+            (5, 0, 128, z_relay.at[1], 7),
+            (4, 0, 64, z_part.at[0], 2),
+            (4, 64, 64, z_part.at[1], 6),
+            (1, 0, 128, z_near.at[0], 1),
+            (7, 0, 128, z_near.at[1], 7),
+            (2, 0, 128, z_near.at[2], 2),
+            (6, 0, 128, z_near.at[3], 6),
+        )[k]
+        return remote(
+            half.at[0, z_rows(chunk, first, count)], target, z_sem.at[k], partner(me, "z", step)
+        )
+
+    def ring_rows(c, p, j):
         if p == 1:
             return pl.ds(pl.multiple_of(lax.div(j, 2) * 8, 8), 8)
-        return pl.ds(pl.multiple_of(j * 32, 32), 32)
+        count = 16 if c == 0 else 32
+        return pl.ds(pl.multiple_of(j * count, count), count)
+
+    def ring_in(c, p):
+        return recv[p].at[c, 0 : SIZE[ORDERS[c][p + 1]] - 1, 0 : (8 if p else 16 if c == 0 else 32)]
 
     def ring_start(c, p):
-        axis = ORDERS[c][p]
-        for o in range(1, 8):
-            target = lax.rem(me[axis] + o, 8)
+        axis = ORDERS[c][p + 1]
+        for o in range(1, SIZE[axis]):
+            target = lax.rem(me[axis] + o, SIZE[axis])
             pltpu.make_async_remote_copy(
-                held[p].at[c, ring_rows(p, target)],
-                recv[p].at[c, o - 1],
+                held[p].at[c, ring_rows(c, p, target)],
+                ring_in(c, p).at[o - 1],
                 ring_sem.at[c, p, 0],
                 ring_sem.at[c, p, 1],
                 device_id=partner(me, axis, o),
@@ -315,29 +351,49 @@
             ).start()
 
     def ring_all(c, p):
-        return remote(recv[p].at[c], recv[p].at[c], ring_sem.at[c, p], sibling)
+        return remote(ring_in(c, p), ring_in(c, p), ring_sem.at[c, p], sibling)
 
     def ring_finish(c, p):
+        axis = ORDERS[c][p + 1]
         ring_all(c, p).wait_recv()
-        total = held[p][c, ring_rows(p, me[ORDERS[c][p]]), :]
-        for o in range(7):
-            total = total + recv[p][c, o]
+        total = held[p][c, ring_rows(c, p, me[axis]), :]
+        count = total.shape[0]
+        for o in range(SIZE[axis] - 1):
+            total = total + recv[p][c, o, 0:count]
         return total
 
     sib_idx_copy(2).wait()
-    v_copy(2).wait()
     for c in THIRDS:
+        v_copy(2, c).wait()
         add_third(2, c)
-        for k in range(4):
-            x_copy(c, k).start()
-    for c in THIRDS:
+        if c == 0:
+            for k in range(6):
+                z_copy(k).start()
+        else:
+            for k in range(4):
+                x_copy(c, k).start()
+
+    def relay_x(c):
         for k, chunk, first in ((0, ahead, 0), (1, behind, 128)):
             x_copy(c, k).wait_recv()
             rows = pl.ds(pl.multiple_of(chunk * 256 + first, 128), 128)
             half[c, rows, :] += relay_in[c, k]
             x_copy(c, 4 + k).start()
+
+    def relay_z():
+        for k, chunk, first in ((0, 2, 0), (1, 6, 64)):
+            z_copy(k).wait_recv()
+            half[0, z_rows(chunk, 0, 128), :] += z_relay[k]
+            z_copy(2 + k).wait_recv()
+            half[0, z_rows(chunk, first, 64), :] += z_part[k]
+            z_copy(6 + k).start()
+
+    relay_x(2)
+    relay_z()
+    relay_x(1)
     own = pl.multiple_of(me["x"] * 256, 256)
-    for c in THIRDS:
+
+    def finish_x(c):
         for k in range(2, 6):
             x_copy(c, k).wait_recv()
         held[0][c, 0:128, :] = half[c, pl.ds(own, 128), :] + near_in[c, 1] + near_in[c, 2]
@@ -345,13 +401,27 @@
             half[c, pl.ds(pl.multiple_of(own + 128, 128), 128), :] + near_in[c, 0] + near_in[c, 3]
         )
         ring_start(c, 0)
-    for c in THIRDS:
-        held[1][c] = ring_finish(c, 0)
+
+    def finish_z():
+        for k in range(4, 8):
+            z_copy(k).wait_recv()
+        total = half[0, z_rows(0, 0, 128), :]
+        for k in range(4):
+            total = total + z_near[k]
+        held[0][0, 0:128, :] = total
+        ring_start(0, 0)
+
+    finish_x(2)
+    finish_z()
+    finish_x(1)
+    for c in (2, 0, 1):
+        total = ring_finish(c, 0)
+        held[1][c, 0 : total.shape[0], :] = total
         ring_start(c, 1)
     last = {}
-    for c in THIRDS:
+    for c in (2, 0, 1):
         total = ring_finish(c, 1)
-        odd = lax.rem(me[ORDERS[c][1]], 2)
+        odd = lax.rem(me[ORDERS[c][2]], 2)
         last[c] = jnp.where(odd == 0, total[0:4], total[4:8])
     grad = jnp.concatenate([last[0], last[1], last[2]], axis=1)
     owner = lax.axis_index("src") * 32 + lax.axis_index("dst")
@@ -360,9 +430,12 @@
     state = as_column(rel_st[...]) + jnp.sum(grad * grad, axis=1, keepdims=True) * (1.0 / 384)
     rel_st_out[...] = as_row(state)
     rel_out[...] = own_rel - 0.1 * grad / jnp.sqrt(state)
-    for c in THIRDS:
+    for k in range(8):
+        z_copy(k).wait_send()
+    for c in ALONG_X:
         for k in range(6):
             x_copy(c, k).wait_send()
+    for c in THIRDS:
         for p in range(2):
             ring_all(c, p).wait_send()
     for copy in ends:
@@ -417,8 +490,8 @@
         pltpu.VMEM((128, 384), F32),
         pltpu.VMEM((1, 128), F32),
         pltpu.VMEM((256, 384), F32),
-        pltpu.VMEM((3, 256, 384), F32),
-        pltpu.VMEM((3, 256, 384), F32),
+        pltpu.VMEM((3, 3, 256, 128), F32),
+        pltpu.VMEM((3, 3, 256, 128), F32),
         pltpu.VMEM((3, 1024, 128), F32),
     ]
     scratch += [
@@ -428,9 +501,12 @@
         pltpu.VMEM((3, 7, 8, 128), F32),
         pltpu.VMEM((3, 256, 128), F32),
         pltpu.VMEM((3, 32, 128), F32),
+        pltpu.VMEM((2, 128, 128), F32),
+        pltpu.VMEM((2, 64, 128), F32),
+        pltpu.VMEM((4, 128, 128), F32),
     ]
-    scratch += [dma((12,)), dma, dma((3, 2)), dma((3, 2)), dma((2, 2)), dma((2, 2)), dma((3, 2)), dma((4, 2))]
-    scratch += [dma((3, 6, 2)), dma((3, 2, 2))]
+    scratch += [dma((12,)), dma, dma((3, 2)), dma((3, 2)), dma((2, 2)), dma((2, 2)), dma((3, 3, 2)), dma((4, 2))]
+    scratch += [dma((3, 6, 2)), dma((8, 2)), dma((3, 2, 2))]
     block = jax.ShapeDtypeStruct((128, 384), F32)
     row = jax.ShapeDtypeStruct((1, 128), F32)
     results = (block, row, block, row)
@@ -439,7 +515,7 @@
         window_kernel,
         out_shape=results,
         in_specs=[hbm] * 11,
-        out_specs=(vmem,) * 6,
+        out_specs=(hbm,) * 4 + (vmem,) * 2,
         scratch_shapes=scratch,
         compiler_params=pltpu.CompilerParams(
             collective_id=0, has_side_effects=True, vmem_limit_bytes=VMEM_LIMIT

time: 69.9 us -> 68.6 us (0.981)
  the two profiles are of different devices: /device:TPU:48 before, /device:TPU:6 now
where the time goes in v5:
time: 68.6 us; the launch traced here: 67.7 us
  Pallas kernels  67.1 us (98%)
    pallas_call x1, Pallas kernels, on_device(): pl.pallas_call(window_kernel, out_shape=results, in_specs=[hbm] * 11, out...  65.3 us
    pallas_call x1, Pallas kernels, on_device(): pl.pallas_call(store_kernel, out_shape=results, in_specs=[hbm] * 6, out_s...  1.81 us

profile of v5, /device:TPU:6, one launch (start us, length us, event | category | flops | bytes accessed | tf_op | source)
XLA Modules:
  0.0 67.7 jit_solution(3700870715293542041)
XLA Ops:
  0.6 65.3 %shard_map.154 = (f32[128,384]{1,0:T(8,128)}, f32[1,128]{1,0:T(1,128)}, f32[128,384]{1,0:T(8,128)}, f32[1,128]{1,0:T(1,128)}, f32[4,384]{1,0:T(4,128)}, /*index=5*/f32[1,4]{1,0:T(1,128)}) custom-call(f32[128,384]{1,0:T(8,128)} %bitcast.15, f32[1,128]{1,0:T(1,128)} %bitcast.21, f32[128,384]{1,0:T(8,128)} %bitcast.16, f32[1,128]{1,0:T(1,128)} %bitcast.22, ...), custom_call_target="tpu_custom_call" | custom-call | tf_op jit(solution)/shard_map/pallas_call | solution.py:514
  65.9 1.8 %shard_map.155 = (f32[128,384]{1,0:T(8,128)}, f32[1,128]{1,0:T(1,128)}, f32[128,384]{1,0:T(8,128)}, f32[1,128]{1,0:T(1,128)}, f32[4,384]{1,0:T(4,128)}, /*index=5*/f32[1,4]{1,0:T(1,128)}) custom-call(f32[128,384]{1,0:T(8,128)} %get-tuple-element.18.refs_0_, f32[1,128]{1,0:T(1,128)} %get-tuple-element.19.refs_1_, f32[128,384]{1,0:T(8,128)} %get-tuple-element.20.refs_2_, ...), custom_call_target="tpu_custom_call" | custom-call | tf_op jit(solution)/shard_map/pallas_call | solution.py:536

commit v6 on v5

--- a/solution.py
+++ b/solution.py
@@ -198,17 +198,22 @@
             both = dot(hot, rhs)
             half[c, rows, :] += both[:, :128] + both[:, 128:]
 
-    def work(t, send_values, send_src):
+    def work(t, wait_src, send_values, send_src):
         rows = idx[t]
         columns = jnp.transpose(rows.astype(F32)).astype(I32)
         s_col, d_col, n_col = columns[:, 0:1], columns[:, 1:2], columns[:, 3:4]
         live = columns[:, 4:5].astype(F32)
         lanes = lax.broadcasted_iota(I32, (256, 256), 1) & 127
-        src_blk, dst_blk = src_in[t], dst_cur[...]
+        dst_blk = dst_cur[...]
         dst_two = split(dst_blk)
-        src_vec = dot(one_hot(lanes == s_col), split(src_blk))
         dst_vec = dot(one_hot(lanes == d_col), dst_two)
         negb = dot(one_hot(lanes[:, :128] == n_col), dst_two[:128]).astype(BF16)
+        s_edge = one_hot(lanes == s_col)
+        subl = lax.broadcasted_iota(I32, (128, 256), 0)
+        s_hot, d_hot, n_hot = (one_hot(subl == rows[i : i + 1]) for i in (0, 1, 3))
+        wait_src()
+        src_blk = src_in[t]
+        src_vec = dot(s_edge, split(src_blk))
         rel = rel_vec[...]
         a = src_vec * rel
         ab = a.astype(BF16)
@@ -226,16 +231,12 @@
         for c in range(3):
             v_own[t, c] = v[:, c * 128 : (c + 1) * 128]
         send_values()
-        subl = lax.broadcasted_iota(I32, (128, 256), 0)
-        s_hot = one_hot(subl == rows[0:1])
         grad_src = dot(jnp.concatenate([s_hot, s_hot], axis=1), split(gprod * rel))
         block, state = adagrad(src_blk, src_st_in[t], grad_src)
         src_new[t] = block
         src_st_new[t] = state
 
         send_src()
-        d_hot = one_hot(subl == rows[1:2])
-        n_hot = one_hot(subl == rows[3:4])
         grad_dst = dot(
             jnp.concatenate([d_hot, d_hot, n_hot, n_hot], axis=1),
             jnp.concatenate([split(gpos * a), split(jnp.concatenate(rows_part, axis=0))], axis=0),
@@ -257,7 +258,7 @@
         send_v(0)
 
     gather_relations(lambda e: r_smem[0, 0, e])
-    work(0, lambda: None, first_sends)
+    work(0, lambda: None, lambda: None, first_sends)
 
     @pl.loop(1, STEPS)
     def _(t):
@@ -267,21 +268,29 @@
         load.start()
         load.wait()
         gather_relations(lambda e: idx_smem[t, 2, e])
-        state_copy(t - 1).wait()
-        block_copy(t - 1).wait()
+
+        def wait_src():
+            state_copy(t - 1).wait()
+            block_copy(t - 1).wait()
 
         def send_src():
             @pl.when(t < 2)
             def _():
                 state_copy(t).start()
                 block_copy(t).start()
+                send_v(t)
 
             @pl.when(t == 2)
             def _():
                 ends[0].start()
                 ends[1].start()
 
-        work(t, lambda: send_v(t), send_src)
+        def send_values():
+            @pl.when(t == 2)
+            def _():
+                send_v(t)
+
+        work(t, wait_src, send_values, send_src)
 
         @pl.when(t == 2)
         def _():

time: 68.6 us -> 69 us (level); the launches traced: 67.7 us -> 68.9 us
  Pallas kernels: 67.1 us -> 68.2 us
    pallas_call x1, Pallas kernels: 65.3 us -> 66.4 us  [on_device(): pl.pallas_call(window_kernel, out_shape=results, in_specs=[hbm] * 11, out...]
where the time goes in v6:
time: 69 us; the launch traced here: 68.9 us
  Pallas kernels  68.2 us (99%)
    pallas_call x1, Pallas kernels, on_device(): pl.pallas_call(window_kernel, out_shape=results, in_specs=[hbm] * 11, out...  66.4 us
    pallas_call x1, Pallas kernels, on_device(): pl.pallas_call(store_kernel, out_shape=results, in_specs=[hbm] * 6, out_s...  1.81 us

profile of v6, /device:TPU:6, one launch (start us, length us, event | category | flops | bytes accessed | tf_op | source)
XLA Modules:
  0.0 68.9 jit_solution(5229721661035527076)
XLA Ops:
  0.6 66.4 %shard_map.154 = (f32[128,384]{1,0:T(8,128)}, f32[1,128]{1,0:T(1,128)}, f32[128,384]{1,0:T(8,128)}, f32[1,128]{1,0:T(1,128)}, f32[4,384]{1,0:T(4,128)}, /*index=5*/f32[1,4]{1,0:T(1,128)}) custom-call(f32[128,384]{1,0:T(8,128)} %bitcast.15, f32[1,128]{1,0:T(1,128)} %bitcast.21, f32[128,384]{1,0:T(8,128)} %bitcast.16, f32[1,128]{1,0:T(1,128)} %bitcast.22, ...), custom_call_target="tpu_custom_call" | custom-call | tf_op jit(solution)/shard_map/pallas_call | solution.py:523
  67.0 1.8 %shard_map.155 = (f32[128,384]{1,0:T(8,128)}, f32[1,128]{1,0:T(1,128)}, f32[128,384]{1,0:T(8,128)}, f32[1,128]{1,0:T(1,128)}, f32[4,384]{1,0:T(4,128)}, /*index=5*/f32[1,4]{1,0:T(1,128)}) custom-call(f32[128,384]{1,0:T(8,128)} %get-tuple-element.18.refs_0_, f32[1,128]{1,0:T(1,128)} %get-tuple-element.19.refs_1_, f32[128,384]{1,0:T(8,128)} %get-tuple-element.20.refs_2_, ...), custom_call_target="tpu_custom_call" | custom-call | tf_op jit(solution)/shard_map/pallas_call | solution.py:545

commit v7 on v5

--- a/solution.py
+++ b/solution.py
@@ -7,7 +7,7 @@
 
 MESH = pl.DeviceIdType.MESH
 F32, BF16, I32 = jnp.float32, jnp.bfloat16, jnp.int32
-ORDERS = (("z", "y", "x"), ("x", "y", "z"), ("x", "z", "y"))
+ORDERS = (("z", "x", "y"), ("x", "z", "y"), ("x", "z", "y"))
 SIZE = {"x": 4, "y": 8, "z": 8}
 THIRDS = (0, 2, 1)
 ALONG_X = (2, 1)
@@ -131,11 +131,11 @@
                 barrier, inc=1, device_id=partner(me, axis, o), device_id_type=MESH
             )
 
-    half[...] = jnp.zeros_like(half)
     for load in loads:
         load.wait()
     block_of = lax.broadcasted_iota(I32, (1, 256), 1) >> 7
-    for t in range(STEPS):
+
+    def pack(t):
         idx_mine[t, 0:1, :] = s_raw[t]
         idx_mine[t, 1:2, :] = d_raw[t]
         idx_mine[t, 2:3, :] = r_raw[t]
@@ -143,6 +143,8 @@
         idx_mine[t, 3:4, 128:256] = n_raw[t, 1:2, :]
         live = jnp.where(block_of < count_smem[0, t], 1, 0)
         idx_mine[t, 4:8, :] = jnp.broadcast_to(live, (4, 256))
+
+    pack(0)
     idx[0] = idx_mine[0]
 
     def remote(source, target, sems, to):
@@ -251,10 +253,13 @@
         enter()
         state_copy(0).start()
         block_copy(0).start()
+        pack(1)
+        pack(2)
         edge_copy(1, EDGES_1).start()
         edge_copy(2, EDGES_2).start()
         sib_idx_copy(0).start()
         send_v(0)
+        half[...] = jnp.zeros_like(half)
 
     gather_relations(lambda e: r_smem[0, 0, e])
     work(0, lambda: None, first_sends)
@@ -331,11 +336,13 @@
     def ring_rows(c, p, j):
         if p == 1:
             return pl.ds(pl.multiple_of(lax.div(j, 2) * 8, 8), 8)
-        count = 16 if c == 0 else 32
-        return pl.ds(pl.multiple_of(j * count, count), count)
+        return pl.ds(pl.multiple_of(j * ring_count(c, p), ring_count(c, p)), ring_count(c, p))
+
+    def ring_count(c, p):
+        return 8 if p else 1024 // SIZE[ORDERS[c][0]] // SIZE[ORDERS[c][1]]
 
     def ring_in(c, p):
-        return recv[p].at[c, 0 : SIZE[ORDERS[c][p + 1]] - 1, 0 : (8 if p else 16 if c == 0 else 32)]
+        return recv[p].at[c, 0 : SIZE[ORDERS[c][p + 1]] - 1, 0 : ring_count(c, p)]
 
     def ring_start(c, p):
         axis = ORDERS[c][p + 1]
@@ -444,8 +451,16 @@
 
 def store_kernel(*refs):
     sources, targets, held, sems = refs[:6], refs[6:12], refs[12:18], refs[18]
-    loads = [pltpu.make_async_copy(sources[i], held[i], sems.at[0, i]) for i in range(6)]
-    stores = [pltpu.make_async_copy(held[i], targets[i], sems.at[1, i]) for i in range(6)]
+    parts = [(i, slice(j * 32, j * 32 + 32)) for j in range(4) for i in (0, 2)]
+    parts += [(i, slice(None)) for i in (1, 3, 4, 5)]
+    loads = [
+        pltpu.make_async_copy(sources[i].at[rows], held[i].at[rows], sems.at[0, n])
+        for n, (i, rows) in enumerate(parts)
+    ]
+    stores = [
+        pltpu.make_async_copy(held[i].at[rows], targets[i].at[rows], sems.at[1, n])
+        for n, (i, rows) in enumerate(parts)
+    ]
     for load in loads:
         load.start()
     for load, store in zip(loads, stores):
@@ -538,7 +553,7 @@
         out_shape=results,
         in_specs=[hbm] * 6,
         out_specs=(hbm,) * 6,
-        scratch_shapes=[pltpu.VMEM(r.shape, F32) for r in results] + [dma((2, 6))],
+        scratch_shapes=[pltpu.VMEM(r.shape, F32) for r in results] + [dma((2, 12))],
         compiler_params=pltpu.CompilerParams(vmem_limit_bytes=VMEM_LIMIT),
     )(*outs)
     return (

time: 68.6 us -> 67.9 us (0.990); the launches traced: 67.7 us -> 67.8 us
  no operation moved by 1% of the time
where the time goes in v7:
time: 67.9 us; the launch traced here: 67.8 us
  Pallas kernels  67.1 us (99%)
    pallas_call x1, Pallas kernels, on_device(): pl.pallas_call(window_kernel, out_shape=results, in_specs=[hbm] * 11, out...  65.3 us
    pallas_call x1, Pallas kernels, on_device(): pl.pallas_call(store_kernel, out_shape=results, in_specs=[hbm] * 6, out_s...  1.8 us

profile of v7, /device:TPU:6, one launch (start us, length us, event | category | flops | bytes accessed | tf_op | source)
XLA Modules:
  0.0 67.8 jit_solution(7620880370412650563)
XLA Ops:
  0.6 65.3 %shard_map.154 = (f32[128,384]{1,0:T(8,128)}, f32[1,128]{1,0:T(1,128)}, f32[128,384]{1,0:T(8,128)}, f32[1,128]{1,0:T(1,128)}, f32[4,384]{1,0:T(4,128)}, /*index=5*/f32[1,4]{1,0:T(1,128)}) custom-call(f32[128,384]{1,0:T(8,128)} %bitcast.15, f32[1,128]{1,0:T(1,128)} %bitcast.21, f32[128,384]{1,0:T(8,128)} %bitcast.16, f32[1,128]{1,0:T(1,128)} %bitcast.22, ...), custom_call_target="tpu_custom_call" | custom-call | tf_op jit(solution)/shard_map/pallas_call | solution.py:529
  65.9 1.8 %shard_map.155 = (f32[128,384]{1,0:T(8,128)}, f32[1,128]{1,0:T(1,128)}, f32[128,384]{1,0:T(8,128)}, f32[1,128]{1,0:T(1,128)}, f32[4,384]{1,0:T(4,128)}, /*index=5*/f32[1,4]{1,0:T(1,128)}) custom-call(f32[128,384]{1,0:T(8,128)} %get-tuple-element.18.refs_0_, f32[1,128]{1,0:T(1,128)} %get-tuple-element.19.refs_1_, f32[128,384]{1,0:T(8,128)} %get-tuple-element.20.refs_2_, ...), custom_call_target="tpu_custom_call" | custom-call | tf_op jit(solution)/shard_map/pallas_call | solution.py:551

commit v8 on v7

--- a/solution.py
+++ b/solution.py
@@ -280,13 +280,19 @@
             def _():
                 state_copy(t).start()
                 block_copy(t).start()
+                send_v(t)
 
             @pl.when(t == 2)
             def _():
                 ends[0].start()
                 ends[1].start()
 
-        work(t, lambda: send_v(t), send_src)
+        def send_values():
+            @pl.when(t == 2)
+            def _():
+                send_v(t)
+
+        work(t, send_values, send_src)
 
         @pl.when(t == 2)
         def _():

time: 67.9 us -> 67.9 us (level)
  no operation moved by 1% of the time
where the time goes in v8:
time: 67.9 us; the launch traced here: 67.8 us
  Pallas kernels  67.1 us (99%)
    pallas_call x1, Pallas kernels, on_device(): pl.pallas_call(window_kernel, out_shape=results, in_specs=[hbm] * 11, out...  65.3 us
    pallas_call x1, Pallas kernels, on_device(): pl.pallas_call(store_kernel, out_shape=results, in_specs=[hbm] * 6, out_s...  1.8 us

profile of v8, /device:TPU:6, one launch (start us, length us, event | category | flops | bytes accessed | tf_op | source)
XLA Modules:
  0.0 67.8 jit_solution(3770684007308413828)
XLA Ops:
  0.6 65.3 %shard_map.154 = (f32[128,384]{1,0:T(8,128)}, f32[1,128]{1,0:T(1,128)}, f32[128,384]{1,0:T(8,128)}, f32[1,128]{1,0:T(1,128)}, f32[4,384]{1,0:T(4,128)}, /*index=5*/f32[1,4]{1,0:T(1,128)}) custom-call(f32[128,384]{1,0:T(8,128)} %bitcast.15, f32[1,128]{1,0:T(1,128)} %bitcast.21, f32[128,384]{1,0:T(8,128)} %bitcast.16, f32[1,128]{1,0:T(1,128)} %bitcast.22, ...), custom_call_target="tpu_custom_call" | custom-call | tf_op jit(solution)/shard_map/pallas_call | solution.py:535
  66.0 1.8 %shard_map.155 = (f32[128,384]{1,0:T(8,128)}, f32[1,128]{1,0:T(1,128)}, f32[128,384]{1,0:T(8,128)}, f32[1,128]{1,0:T(1,128)}, f32[4,384]{1,0:T(4,128)}, /*index=5*/f32[1,4]{1,0:T(1,128)}) custom-call(f32[128,384]{1,0:T(8,128)} %get-tuple-element.18.refs_0_, f32[1,128]{1,0:T(1,128)} %get-tuple-element.19.refs_1_, f32[128,384]{1,0:T(8,128)} %get-tuple-element.20.refs_2_, ...), custom_call_target="tpu_custom_call" | custom-call | tf_op jit(solution)/shard_map/pallas_call | solution.py:557
